TPU v7x, 32 devices: a whole 2x2x4 slice. The times are simulated.
32 devices in a mesh: dp: 2 (over y), pipe: 4 (over z), expert: 4 (over x, core).
Axes of the slice: x: 2, y: 2, z: 4, core: 2. Of those that a mesh axis runs over, the one named last changes fastest.
Arguments:
- fresh: bfloat16 [512, 6144], P(('dp', 'expert')), may hold values from -6 to 6
- cotangent: bfloat16 [512, 6144], P(('dp', 'expert')), may hold values from -6 to 6
- prev_out: bfloat16 [4, 512, 6144], P('pipe', ('dp', 'expert')), may hold values from -6 to 6
- prev_grad: bfloat16 [4, 512, 6144], P('pipe', ('dp', 'expert')), may hold values from -6 to 6
- saved_in: bfloat16 [4, 512, 6144], P('pipe', ('dp', 'expert')), may hold values from -6 to 6
- route_fwd: int32 [4, 512, 2], P('pipe', ('dp', 'expert')), may hold values from 0 to 3, all different within a row; in each aligned block of 64 rows (0 to 63, 64 to 127, ..., all dimensions but the last counted through in order) at most 64 rows name the same one
- route_bwd: int32 [4, 512, 2], P('pipe', ('dp', 'expert')), may hold values from 0 to 3, all different within a row; in each aligned block of 64 rows (0 to 63, 64 to 127, ..., all dimensions but the last counted through in order) at most 64 rows name the same one
- router: bfloat16 [4, 6144, 4], P('pipe'), may hold values from -0.078125 to 0.078125
- gate_up: bfloat16 [4, 4, 6144, 256], P('pipe', 'expert'), may hold values from -0.078125 to 0.078125
- down: bfloat16 [4, 4, 128, 6144], P('pipe', 'expert'), may hold values from -0.5 to 0.5
Outputs:
- section_out: bfloat16 [4, 512, 6144], P('pipe', ('dp', 'expert'))
- input_grad: bfloat16 [4, 512, 6144], P('pipe', ('dp', 'expert'))
- grad_gate_up: bfloat16 [4, 4, 6144, 256], P('pipe', 'expert', 'dp')
- grad_down: bfloat16 [4, 4, 128, 6144], P('pipe', 'expert', None, 'dp')
- grad_router: float32 [4, 6144, 4], P('pipe', ('dp', 'expert'))
Inputs may be any that keep to these rules, and one draw needn't show every extreme that they name: `route_fwd`: each row names two different experts; in the 64 rows of one device no expert is named by more than 64 rows, and some expert reaches 64. `route_bwd`: each row names two different experts; in the 64 rows of one device no expert is named by more than 64 rows, and some expert reaches 64.
All inputs are finite; a program needn't handle non-finite values.
Results may differ from a plain program's by a relative error of at most 0.015.
Values may be sent and summed in bfloat16 or wider, within the bound.
A program may use at most 128 MiB of HBM per device.

v0:
```python
import jax
import jax.numpy as jnp
from jax import lax
from jax.sharding import PartitionSpec as P

EPSILON = 1e-05


def passed_along(x, axis, by):
    length = lax.axis_size(axis)
    pairs = [(i, i + by) for i in range(length) if 0 <= i + by < length]
    return lax.ppermute(x, axis, pairs)


def contract_rows(first_operand, second_operand):
    return lax.dot_general(
        first_operand, second_operand, (((0,), (0,)), ((), ())), preferred_element_type=jnp.float32
    )


def contract_cols(first_operand, second_operand):
    return lax.dot_general(
        first_operand, second_operand, (((1,), (1,)), ((), ())), preferred_element_type=jnp.float32
    )


def exact_rows(first_operand, second_operand):
    return lax.dot_general(
        first_operand,
        second_operand,
        (((0,), (0,)), ((), ())),
        precision=lax.Precision.HIGHEST,
        preferred_element_type=jnp.float32,
    )


def normalize(values_in):
    values = values_in.astype(jnp.float32)
    spread = jnp.sqrt(jnp.mean(values * values, axis=-1, keepdims=True) + EPSILON)
    return (values / spread, spread)


def gate_pair(normed, router_w, routes):
    experts = router_w.shape[1]
    logits = jnp.dot(normed, router_w, preferred_element_type=jnp.float32)
    onehot = (routes[:, :, None] == jnp.arange(experts, dtype=jnp.int32)[None, None, :]).astype(
        jnp.float32
    )
    chosen = jnp.sum(onehot * logits[:, None, :], axis=2)
    first_gate = jax.nn.sigmoid(chosen[:, 0] - chosen[:, 1])
    second_gate = jax.nn.sigmoid(chosen[:, 1] - chosen[:, 0])
    return (first_gate, second_gate, onehot)


def route_rows(routes, my_replica, replicas, owners, experts, per_peer):
    flattened = routes.reshape(-1)
    onehot = (flattened[:, None] == jnp.arange(experts, dtype=jnp.int32)[None, :]).astype(jnp.int32)
    position = jnp.sum((jnp.cumsum(onehot, axis=0) - onehot) * onehot, axis=1)
    replica = (my_replica + position) % replicas
    target = replica * owners + flattened
    return (target * per_peer + position // replicas).reshape(routes.shape)


def expert_forward(inputs, gate_up_w, down_w):
    hidden_width = down_w.shape[0]
    projected = jnp.dot(inputs, gate_up_w, preferred_element_type=jnp.float32)
    pre_gate = projected[:, :hidden_width]
    pre_up = projected[:, hidden_width:]
    hidden = (pre_gate * jax.nn.sigmoid(pre_gate) * pre_up).astype(jnp.bfloat16)
    return jnp.dot(hidden, down_w, preferred_element_type=jnp.float32).astype(jnp.bfloat16)


def expert_backward(inputs, upstream, weight, gate_up_w, down_w):
    hidden_width = down_w.shape[0]
    projected = jnp.dot(inputs, gate_up_w, preferred_element_type=jnp.float32)
    pre_gate = projected[:, :hidden_width]
    pre_up = projected[:, hidden_width:]
    sigmoid_gate = jax.nn.sigmoid(pre_gate)
    active = pre_gate * sigmoid_gate
    hidden = (active * pre_up).astype(jnp.bfloat16)
    output = jnp.dot(hidden, down_w, preferred_element_type=jnp.float32).astype(jnp.bfloat16)
    gate_grad = jnp.sum(upstream.astype(jnp.float32) * output.astype(jnp.float32), axis=1).astype(
        jnp.bfloat16
    )
    out_grad = (weight.astype(jnp.float32)[:, None] * upstream.astype(jnp.float32)).astype(
        jnp.bfloat16
    )
    hidden_grad = contract_cols(out_grad, down_w)
    grad_g = hidden_grad * pre_up * sigmoid_gate * (1.0 + pre_gate * (1.0 - sigmoid_gate))
    grad_u = hidden_grad * active
    pre_grad = jnp.concatenate([grad_g, grad_u], axis=1).astype(jnp.bfloat16)
    row_grad = contract_cols(pre_grad, gate_up_w).astype(jnp.bfloat16)
    gate_up_part = contract_rows(inputs, pre_grad)
    down_part = contract_rows(hidden, out_grad)
    return (row_grad, gate_grad, gate_up_part, down_part)


def shards(
    fresh, cotangent, prev_out, prev_grad, saved_in, route_fwd, route_bwd, router, gate_up, down
):
    section_index = lax.axis_index("pipe")
    sections = lax.axis_size("pipe")
    replicas = lax.axis_size("dp")
    owners = lax.axis_size("expert")
    my_replica = lax.axis_index("dp")
    arrived = passed_along(prev_out[0], "pipe", 1)
    returned = passed_along(prev_grad[0], "pipe", -1)
    inputs_fwd = jnp.where(section_index == 0, fresh, arrived)
    upstream = jnp.where(section_index == sections - 1, cotangent, returned)
    inputs_bwd = saved_in[0]
    router_w = router[0]
    gate_up_w = gate_up[0, 0]
    down_w = down[0, 0]
    tokens = fresh.shape[0]
    model_width = fresh.shape[1]
    experts = router_w.shape[1]
    capacity = min(tokens, 4 * tokens // experts)
    per_peer = (capacity + replicas - 1) // replicas
    peer_count = replicas * owners
    buffer_rows = peer_count * per_peer
    line_index = jnp.arange(buffer_rows, dtype=jnp.int32)[:, None]

    def trade_rows(payload):
        return lax.all_to_all(payload, ("dp", "expert"), split_axis=0, concat_axis=0, tiled=True)

    def trade_pair(rows_part, column):
        return (
            lax.all_to_all(rows_part, ("dp", "expert"), split_axis=0, concat_axis=0, tiled=True),
            lax.all_to_all(column, ("dp", "expert"), split_axis=0, concat_axis=0, tiled=True),
        )

    unit_fwd, spread_fwd = normalize(inputs_fwd)
    packed_fwd = unit_fwd.astype(jnp.bfloat16)
    gates_fwd = gate_pair(packed_fwd, router_w, route_fwd[0])
    rows_fwd = route_rows(route_fwd[0], my_replica, replicas, owners, experts, per_peer)
    pick_first = (line_index == rows_fwd[None, :, 0]).astype(jnp.bfloat16)
    pick_second = (line_index == rows_fwd[None, :, 1]).astype(jnp.bfloat16)
    outbound = jnp.dot(
        pick_first + pick_second, packed_fwd, preferred_element_type=jnp.float32
    ).astype(jnp.bfloat16)
    received = trade_rows(outbound.reshape(peer_count, per_peer, model_width)).reshape(
        buffer_rows, model_width
    )
    results = expert_forward(received, gate_up_w, down_w)
    returned_rows = trade_rows(results.reshape(peer_count, per_peer, model_width)).reshape(
        buffer_rows, model_width
    )
    first_out = contract_rows(pick_first, returned_rows)
    second_out = contract_rows(pick_second, returned_rows)
    section_value = (
        inputs_fwd.astype(jnp.float32)
        + gates_fwd[0][:, None] * first_out
        + gates_fwd[1][:, None] * second_out
    )
    section_out = section_value.astype(jnp.bfloat16)
    unit_bwd, spread_bwd = normalize(inputs_bwd)
    packed_bwd = unit_bwd.astype(jnp.bfloat16)
    first_bwd, second_bwd, onehot_bwd = gate_pair(packed_bwd, router_w, route_bwd[0])
    rows_bwd = route_rows(route_bwd[0], my_replica, replicas, owners, experts, per_peer)
    pick_one = (line_index == rows_bwd[None, :, 0]).astype(jnp.bfloat16)
    pick_two = (line_index == rows_bwd[None, :, 1]).astype(jnp.bfloat16)
    joined = jnp.concatenate([packed_bwd, upstream], axis=1)
    outbound_rows = jnp.dot(pick_one + pick_two, joined, preferred_element_type=jnp.float32).astype(
        jnp.bfloat16
    )
    weight_rows = jnp.dot(
        pick_one.astype(jnp.float32), first_bwd, precision=lax.Precision.HIGHEST
    ) + jnp.dot(pick_two.astype(jnp.float32), second_bwd, precision=lax.Precision.HIGHEST)
    got_rows, got_weight = trade_pair(
        outbound_rows.reshape(peer_count, per_peer, 2 * model_width),
        weight_rows.astype(jnp.bfloat16).reshape(peer_count, per_peer),
    )
    got_rows = got_rows.reshape(buffer_rows, 2 * model_width)
    row_grad, gate_grad, gate_up_part, down_part = expert_backward(
        got_rows[:, :model_width],
        got_rows[:, model_width:],
        got_weight.reshape(-1),
        gate_up_w,
        down_w,
    )
    back_rows, back_gate = trade_pair(
        row_grad.reshape(peer_count, per_peer, model_width), gate_grad.reshape(peer_count, per_peer)
    )
    back_rows = back_rows.reshape(buffer_rows, model_width)
    back_gate = back_gate.reshape(-1).astype(jnp.float32)
    normed_grad = contract_rows(pick_one + pick_two, back_rows)
    gate_first = exact_rows(pick_one.astype(jnp.float32), back_gate)
    gate_second = exact_rows(pick_two.astype(jnp.float32), back_gate)
    logit_step = first_bwd * second_bwd * (gate_first - gate_second)
    logit_grad = (onehot_bwd[:, 0, :] - onehot_bwd[:, 1, :]) * logit_step[:, None]
    normed_grad = normed_grad + jnp.dot(
        logit_grad, router_w.astype(jnp.float32).T, precision=lax.Precision.HIGHEST
    )
    router_part = exact_rows(packed_bwd.astype(jnp.float32), logit_grad)
    inner_mean = jnp.mean(normed_grad * unit_bwd, axis=1, keepdims=True)
    grad_value = upstream.astype(jnp.float32) + (normed_grad - unit_bwd * inner_mean) / spread_bwd
    input_grad = grad_value.astype(jnp.bfloat16)
    grad_gate_up = lax.psum_scatter(
        gate_up_part.astype(jnp.bfloat16), "dp", scatter_dimension=0, tiled=True
    )
    grad_down = lax.psum_scatter(
        down_part.astype(jnp.bfloat16), "dp", scatter_dimension=1, tiled=True
    )
    grad_router = lax.psum_scatter(router_part, ("dp", "expert"), scatter_dimension=0, tiled=True)
    return (
        section_out[None],
        input_grad[None],
        grad_gate_up[None, None],
        grad_down[None, None],
        grad_router[None],
    )


def solution(mesh):
    placed = (
        P(("dp", "expert"), None),
        P(("dp", "expert"), None),
        P("pipe", ("dp", "expert"), None),
        P("pipe", ("dp", "expert"), None),
        P("pipe", ("dp", "expert"), None),
        P("pipe", ("dp", "expert"), None),
        P("pipe", ("dp", "expert"), None),
        P("pipe", None, None),
        P("pipe", "expert", None, None),
        P("pipe", "expert", None, None),
    )
    return jax.shard_map(
        shards,
        mesh=mesh,
        in_specs=placed,
        out_specs=(
            P("pipe", ("dp", "expert"), None),
            P("pipe", ("dp", "expert"), None),
            P("pipe", "expert", "dp", None),
            P("pipe", "expert", None, "dp"),
            P("pipe", ("dp", "expert"), None),
        ),
        check_vma=False,
    )
```

profile of v0, /device:TPU:0, one launch (start us, length us, event | category | flops | bytes accessed | tf_op | source)
XLA Modules:
  0.0 332.4 jit_solution(189519160720842368)
XLA Ops:
  12.7 1.5 fusion.65
  15.3 5.2 %all-to-all-start.2 = ((bf16[8,1,32]{2,1,0:T(2,128)(2,1)}), bf16[8,1,32]{2,1,0:T(2,128)(2,1)S(1)}, u32[]{:S(2)}, u32[]{:S(2)}) async-start(bf16[8,1,32]{2,1,0:T(2,128)(2,1)} %all_to_all.29), calls=%async_computation.2 | async-start | bytes 8192 | tf_op jit(solution)/shard_map/all_to_all | solution.py:129
  23.1 19.5 %collective-permute-done.1 = bf16[64,6144]{1,0:T(8,128)(2,1)} collective-permute-done((bf16[64,6144]{1,0:T(8,128)(2,1)}, bf16[64,6144]{1,0:T(8,128)(2,1)}, u32[]{:S(2)}, u32[]{:S(2)}) %collective-permute-start.1) | collective-permute-done | bytes 786464 | tf_op jit(solution)/shard_map/ppermute | solution.py:12
  44.7 4.4 %convolution_convert_fusion = bf16[256,12288]{1,0:T(8,128)(2,1)} fusion(bf16[64,6144]{1,0:T(8,128)(2,1)S(1)} %broadcast_select_fusion, bf16[64,6144]{1,0:T(8,128)(2,1)S(1)} %fusion.87, s32[64]{0:T(128)S(1)} %get-tuple-element.10, s32[64]{0:T(128)S(1)} %get-tuple-element.11), kind=kOutput, calls=%fused_computation | convolution fusion | flops 409075712 | bytes 7864832 | tf_op jit(solution)/shard_map/dot_general | solution.py:163
  49.2 4.7 %all-to-all-start.3 = ((bf16[8,32,12288]{2,1,0:T(8,128)(2,1)}), bf16[8,32,12288]{2,1,0:T(8,128)(2,1)}, u32[]{:S(2)}, u32[]{:S(2)}) async-start(bf16[8,32,12288]{2,1,0:T(8,128)(2,1)} %bitcast.109), calls=%async_computation.3 | async-start | bytes 12582912 | tf_op jit(solution)/shard_map/all_to_all | solution.py:128
  53.9 4.4 %collective-permute-start = (bf16[64,6144]{1,0:T(8,128)(2,1)}, bf16[64,6144]{1,0:T(8,128)(2,1)}, u32[]{:S(2)}, u32[]{:S(2)}) collective-permute-start(bf16[64,6144]{1,0:T(8,128)(2,1)} %bitcast.121), channel_id=1, source_target_pairs={{0,4},{4,8},{8,12},{1,5},{5,9},{9,13},{2,6},{6,10},{10,14},{3,7},{... | collective-permute-start | bytes 2359304 | tf_op jit(solution)/shard_map/ppermute | solution.py:12
  58.5 16.6 %collective-permute-done = bf16[64,6144]{1,0:T(8,128)(2,1)} collective-permute-done((bf16[64,6144]{1,0:T(8,128)(2,1)}, bf16[64,6144]{1,0:T(8,128)(2,1)}, u32[]{:S(2)}, u32[]{:S(2)}) %collective-permute-start) | collective-permute-done | bytes 786464 | tf_op jit(solution)/shard_map/ppermute | solution.py:12
  75.1 2.4 fusion.18
  77.5 48.1 %all-to-all-done.3 = bf16[8,32,12288]{2,1,0:T(8,128)(2,1)} async-done(((bf16[8,32,12288]{2,1,0:T(8,128)(2,1)}), bf16[8,32,12288]{2,1,0:T(8,128)(2,1)}, u32[]{:S(2)}, u32[]{:S(2)}) %all-to-all-start.3) | async-done | bytes 6291488 | tf_op jit(solution)/shard_map/all_to_all | solution.py:128
  125.5 3.0 fusion.7
  128.5 2.9 multiply_convert_fusion.2
  131.5 3.0 fusion.15
  135.1 3.3 all-to-all-start.5
  138.5 3.9 %convolution_convert_fusion.5 = bf16[256,6144]{1,0:T(8,128)(2,1)} fusion(s32[64]{0:T(128)S(1)} %get-tuple-element.17, s32[64]{0:T(128)S(1)} %get-tuple-element.16, bf16[64,6144]{1,0:T(8,128)(2,1)} %get-tuple-element.6, f32[64]{0:T(128)S(1)} %add_sqrt_fusion.1), kind=kOutput, calls=%fused_computation.8 | convolution fusion | flops 204210176 | bytes 3932928 | tf_op jit(solution)/shard_map/dot_general | solution.py:138
  143.0 4.4 %all-to-all-start = ((bf16[8,32,6144]{2,1,0:T(8,128)(2,1)}), bf16[8,32,6144]{2,1,0:T(8,128)(2,1)}, u32[]{:S(2)}, u32[]{:S(2)}) async-start(bf16[8,32,6144]{2,1,0:T(8,128)(2,1)} %bitcast.112), calls=%async_computation | async-start | bytes 6291456 | tf_op jit(solution)/shard_map/all_to_all | solution.py:124
  147.9 4.6 %fusion.84 = f32[6144,4]{1,0:T(8,128)} fusion(f32[64,2,4]{0,2,1:T(4,128)S(1)} %fusion.69, f32[64]{0:T(128)S(1)} %fusion.28, bf16[1,64,6144]{2,1,0:T(8,128)(2,1)} %param.14, f32[64]{0:T(128)S(1)} %add_sqrt_fusion), kind=kOutput, calls=%fused_computation.146 | convolution fusion | flops 20054528 | bytes 887296
  152.8 3.9 %convolution_convert_fusion.6 = bf16[128,6144]{1,0:T(8,128)(2,1)} fusion(bf16[256,128]{1,0:T(8,128)(2,1)S(1)} %get-tuple-element.9, f32[256]{0:T(256)S(1)} %reshape.156, bf16[256,12288]{1,0:T(8,128)(2,1)} %bitcast.25), kind=kOutput, calls=%fused_computation.9 | convolution fusion | flops 408158208 | bytes 4785152 | tf_op jit(solution)/shard_map/dot_general | solution.py:16
  156.7 36.3 %all-to-all-done = bf16[8,32,6144]{2,1,0:T(8,128)(2,1)} async-done(((bf16[8,32,6144]{2,1,0:T(8,128)(2,1)}), bf16[8,32,6144]{2,1,0:T(8,128)(2,1)}, u32[]{:S(2)}, u32[]{:S(2)}) %all-to-all-start) | async-done | bytes 3145760 | tf_op jit(solution)/shard_map/all_to_all | solution.py:124
  193.0 3.0 fusion.9
  196.0 2.6 convolution_convert_fusion.4
  198.6 4.5 %all-to-all-start.1 = ((bf16[8,32,6144]{2,1,0:T(8,128)(2,1)}), bf16[8,32,6144]{2,1,0:T(8,128)(2,1)}, u32[]{:S(2)}, u32[]{:S(2)}) async-start(bf16[8,32,6144]{2,1,0:T(8,128)(2,1)} %bitcast.111), calls=%async_computation.1 | async-start | bytes 6291456 | tf_op jit(solution)/shard_map/all_to_all | solution.py:124
  203.1 4.6 %convolution_convert_fusion.1 = bf16[6144,256]{1,0:T(8,128)(2,1)} fusion(bf16[256,12288]{1,0:T(8,128)(2,1)} %bitcast.25, bf16[256,128]{1,0:T(8,128)(2,1)S(1)} %get-tuple-element.8, bf16[256,128]{1,0:T(8,128)(2,1)S(1)} %get-tuple-element.7), kind=kOutput, calls=%fused_computation.3 | convolution fusion | flops 807141376 | bytes 6422528 | tf_op jit(solution)/shard_map/dot_general | solution.py:16
  207.8 2.7 convolution_convert_fusion.3
  210.4 33.7 %all-to-all-done.1 = bf16[8,32,6144]{2,1,0:T(8,128)(2,1)} async-done(((bf16[8,32,6144]{2,1,0:T(8,128)(2,1)}), bf16[8,32,6144]{2,1,0:T(8,128)(2,1)}, u32[]{:S(2)}, u32[]{:S(2)}) %all-to-all-start.1) | async-done | bytes 3145760 | tf_op jit(solution)/shard_map/all_to_all | solution.py:124
  244.1 7.0 %all-to-all-start.4 = ((bf16[8,32,6144]{2,1,0:T(8,128)(2,1)}), bf16[8,32,6144]{2,1,0:T(8,128)(2,1)}, u32[]{:S(2)}, u32[]{:S(2)}) async-start(bf16[8,32,6144]{2,1,0:T(8,128)(2,1)} %bitcast.110), calls=%async_computation.4 | async-start | bytes 6291456 | tf_op jit(solution)/shard_map/all_to_all | solution.py:128
  251.1 1.5 fusion.67
  252.7 2.7 convolution_multiply_fusion
  255.4 3.6 %fusion.4 = bf16[1,64,6144]{2,1,0:T(8,128)(2,1)} fusion(f32[64,6144]{1,0:T(8,128)S(1)} %convolution_multiply_fusion, bf16[256,6144]{1,0:T(8,128)(2,1)} %bitcast.11, bf16[64,6144]{1,0:T(8,128)(2,1)S(1)} %copy-done.4, f32[64]{0:T(128)S(1)} %get-tuple-element.14, s32[64]{0:T(128)S(1)} %get-tuple-element.16), kind=kOutput, calls=%fused_computation.16 | convolution fusion | flops 203309056 | bytes 6291968 | tf_op jit(solution)/shard_map/dot_general | solution.py:16
  259.1 1.7 copy.98
  260.8 32.7 %all-to-all-done.4 = bf16[8,32,6144]{2,1,0:T(8,128)(2,1)} async-done(((bf16[8,32,6144]{2,1,0:T(8,128)(2,1)}), bf16[8,32,6144]{2,1,0:T(8,128)(2,1)}, u32[]{:S(2)}, u32[]{:S(2)}) %all-to-all-start.4) | async-done | bytes 3145760 | tf_op jit(solution)/shard_map/all_to_all | solution.py:128
  293.5 2.7 fusion.45
  298.7 27.1 %reduce-scatter.6.cloned.1.call-done = bf16[3072,256]{1,0:T(8,128)(2,1)} async-done(((bf16[6144,256]{1,0:T(8,128)(2,1)}), bf16[3072,256]{1,0:T(8,128)(2,1)}) %reduce-scatter.6.cloned.1.call-update) | async-done | bytes 1572880 | tf_op jit(solution)/shard_map/reduce_scatter | solution.py:198
  (72 shorter events, 16.1 us)
Async XLA Ops:
  7.2 118.4 %copy-start = (bf16[1,1,6144,256]{3,2,1,0:T(8,128)(2,1)S(1)}, bf16[1,1,6144,256]{3,2,1,0:T(8,128)(2,1)}, u32[]{:S(2)}) copy-start(bf16[1,1,6144,256]{3,2,1,0:T(8,128)(2,1)} %param.18) | copy-start | bytes 9437188
  11.2 3.0 copy-start.7
  15.3 33.9 %all-to-all-start.2 = ((bf16[8,1,32]{2,1,0:T(2,128)(2,1)}), bf16[8,1,32]{2,1,0:T(2,128)(2,1)S(1)}, u32[]{:S(2)}, u32[]{:S(2)}) async-start(bf16[8,1,32]{2,1,0:T(2,128)(2,1)} %all_to_all.29), calls=%async_computation.2 | async-start | bytes 8192 | tf_op jit(solution)/shard_map/all_to_all | solution.py:129
  20.5 22.2 %collective-permute-start.1 = (bf16[64,6144]{1,0:T(8,128)(2,1)}, bf16[64,6144]{1,0:T(8,128)(2,1)}, u32[]{:S(2)}, u32[]{:S(2)}) collective-permute-start(bf16[64,6144]{1,0:T(8,128)(2,1)} %bitcast.120), channel_id=1, source_target_pairs={{4,0},{8,4},{12,8},{5,1},{9,5},{13,9},{6,2},{10,6},{14,10},{7,3},{... | collective-permute-start | bytes 2359304 | tf_op jit(solution)/shard_map/ppermute | solution.py:12
  43.9 0.9 copy-start.1
  49.2 76.3 %all-to-all-start.3 = ((bf16[8,32,12288]{2,1,0:T(8,128)(2,1)}), bf16[8,32,12288]{2,1,0:T(8,128)(2,1)}, u32[]{:S(2)}, u32[]{:S(2)}) async-start(bf16[8,32,12288]{2,1,0:T(8,128)(2,1)} %bitcast.109), calls=%async_computation.3 | async-start | bytes 12582912 | tf_op jit(solution)/shard_map/all_to_all | solution.py:128
  53.9 21.1 %collective-permute-start = (bf16[64,6144]{1,0:T(8,128)(2,1)}, bf16[64,6144]{1,0:T(8,128)(2,1)}, u32[]{:S(2)}, u32[]{:S(2)}) collective-permute-start(bf16[64,6144]{1,0:T(8,128)(2,1)} %bitcast.121), channel_id=1, source_target_pairs={{0,4},{4,8},{8,12},{1,5},{5,9},{9,13},{2,6},{6,10},{10,14},{3,7},{... | collective-permute-start | bytes 2359304 | tf_op jit(solution)/shard_map/ppermute | solution.py:12
  125.5 3.0 copy-start.5
  135.1 7.8 %all-to-all-start.5 = ((bf16[8,1,32]{2,1,0:T(2,128)(2,1)}), bf16[8,1,32]{2,1,0:T(2,128)(2,1)S(1)}, u32[]{:S(2)}, u32[]{:S(2)}) async-start(bf16[8,1,32]{2,1,0:T(2,128)(2,1)} %convert_element_type.166), calls=%async_computation.5 | async-start | bytes 8192 | tf_op jit(solution)/shard_map/all_to_all | solution.py:129
  143.0 50.0 %all-to-all-start = ((bf16[8,32,6144]{2,1,0:T(8,128)(2,1)}), bf16[8,32,6144]{2,1,0:T(8,128)(2,1)}, u32[]{:S(2)}, u32[]{:S(2)}) async-start(bf16[8,32,6144]{2,1,0:T(8,128)(2,1)} %bitcast.112), calls=%async_computation | async-start | bytes 6291456 | tf_op jit(solution)/shard_map/all_to_all | solution.py:124
  147.4 111.6 %reduce-scatter.10.cloned.1.call-start = ((), (), s32[]{:S(2)}) async-start(), calls=%async_computation.11 | async-start | bytes 3538944
  152.6 146.2 %reduce-scatter.8.cloned.1.call-start = ((), (), s32[]{:S(2)}) async-start(), calls=%async_computation.10 | async-start | bytes 2359296 | tf_op jit(solution)/shard_map/reduce_scatter | solution.py:201
  193.0 3.0 copy-start.6
  198.6 45.5 %all-to-all-start.1 = ((bf16[8,32,6144]{2,1,0:T(8,128)(2,1)}), bf16[8,32,6144]{2,1,0:T(8,128)(2,1)}, u32[]{:S(2)}, u32[]{:S(2)}) async-start(bf16[8,32,6144]{2,1,0:T(8,128)(2,1)} %bitcast.111), calls=%async_computation.1 | async-start | bytes 6291456 | tf_op jit(solution)/shard_map/all_to_all | solution.py:124
  203.1 122.8 %reduce-scatter.6.cloned.1.call-start = ((), (), s32[]{:S(2)}) async-start(), calls=%async_computation.9 | async-start | bytes 4718592 | tf_op jit(solution)/shard_map/reduce_scatter | solution.py:198
  244.1 7.0 %copy-start.9 = (bf16[1,6144,4]{1,2,0:T(4,128)(2,1)S(1)}, bf16[1,6144,4]{1,2,0:T(4,128)(2,1)}, u32[]{:S(2)}) copy-start(bf16[1,6144,4]{1,2,0:T(4,128)(2,1)} %param.17) | copy-start | bytes 147460
  244.1 49.4 %all-to-all-start.4 = ((bf16[8,32,6144]{2,1,0:T(8,128)(2,1)}), bf16[8,32,6144]{2,1,0:T(8,128)(2,1)}, u32[]{:S(2)}, u32[]{:S(2)}) async-start(bf16[8,32,6144]{2,1,0:T(8,128)(2,1)} %bitcast.110), calls=%async_computation.4 | async-start | bytes 6291456 | tf_op jit(solution)/shard_map/all_to_all | solution.py:128
  251.1 1.5 copy-start.8
  252.6 2.8 copy-start.4
  293.5 2.7 copy-start.3
  296.2 1.2 copy-start.2
Sparse Core Ops, SparseCore 0:
  152.7 53.3 reduce-scatter.9
  209.0 51.3 reduce-scatter.7
  263.1 62.6 reduce-scatter.5
where the time goes:
time: 334 us; the launch traced here: 332 us
  waiting for transfers between devices  215 us (64%)
  matrix products  52.5 us (16%)
  starting transfers between devices  35.1 us (11%)
  between operations  14 us (4%)
  other arithmetic  9.43 us (3%)
  local copies, waits for them, and re-layouts  6.67 us (2%)
    all_to_all x2, waiting for transfers between devices, trade_pair(): lax.all_to_all(rows_part, ('dp', 'expert'), split_axis=0, concat_axis=0,...  80.8 us
    all_to_all x2, waiting for transfers between devices, trade_rows(): lax.all_to_all(payload, ('dp', 'expert'), split_axis=0, concat_axis=0, ti...  69.9 us
    ppermute x2, waiting for transfers between devices, passed_along(): return lax.ppermute(x, axis, pairs)  36.1 us
    reduce_scatter x1, waiting for transfers between devices, shards(): lax.psum_scatter(gate_up_part.astype(jnp.bfloat16), 'dp', scatter_dimensi...  27.1 us
    dot_general x5, matrix products, contract_rows(): lax.dot_general(first_operand, second_operand, (((0,), (0,)), ((), ())),...  17.5 us
    all_to_all x2, starting transfers between devices, trade_pair(): lax.all_to_all(rows_part, ('dp', 'expert'), split_axis=0, concat_axis=0,...  11.7 us
    all_to_all x2, starting transfers between devices, trade_rows(): lax.all_to_all(payload, ('dp', 'expert'), split_axis=0, concat_axis=0, ti...  8.91 us
    all_to_all x2, starting transfers between devices, trade_pair(): lax.all_to_all(column, ('dp', 'expert'), split_axis=0, concat_axis=0, til...  8.48 us
  transfers between devices with their start and end apart: 11, of which 8 were waited for; matrix products, arithmetic and copies ran while one was open for 15% of the time, Pallas kernels for 0%

commit v1 on v0

v1 whole, which is shorter than its diff:
```python
import jax
import jax.numpy as jnp
from jax import lax
from jax.sharding import PartitionSpec as P

EPSILON = 1e-05


def passed_along(x, axis, by):
    length = lax.axis_size(axis)
    pairs = [(i, i + by) for i in range(length) if 0 <= i + by < length]
    return lax.ppermute(x, axis, pairs)


def dot(a, b, ca, cb):
    return lax.dot_general(a, b, (((ca,), (cb,)), ((), ())), preferred_element_type=jnp.float32)


def normalize(values_in):
    values = values_in.astype(jnp.float32)
    spread = jnp.sqrt(jnp.mean(values * values, axis=-1, keepdims=True) + EPSILON)
    return (values / spread, spread)


def gates(normed, router_w, routes):
    experts = router_w.shape[1]
    logits = jnp.dot(normed, router_w, preferred_element_type=jnp.float32)
    onehot = (routes[:, :, None] == jnp.arange(experts, dtype=jnp.int32)[None, None, :]).astype(
        jnp.float32
    )
    chosen = jnp.sum(onehot * logits[:, None, :], axis=2)
    first = jax.nn.sigmoid(chosen[:, 0] - chosen[:, 1])
    second = jax.nn.sigmoid(chosen[:, 1] - chosen[:, 0])
    return first, second, onehot


def shards(
    fresh, cotangent, prev_out, prev_grad, saved_in, route_fwd, route_bwd, router, gate_up, down
):
    section = lax.axis_index("pipe")
    sections = lax.axis_size("pipe")
    me = lax.axis_index("expert")
    arrived = passed_along(prev_out[0], "pipe", 1)
    returned = passed_along(prev_grad[0], "pipe", -1)
    inputs_fwd = jnp.where(section == 0, fresh, arrived)
    upstream = jnp.where(section == sections - 1, cotangent, returned)
    inputs_bwd = saved_in[0]
    router_w, gate_up_w, down_w = router[0], gate_up[0, 0], down[0, 0]
    width = down_w.shape[0]
    model = fresh.shape[1]
    experts = router_w.shape[1]

    def gather(x):
        return lax.all_gather(x, "expert", axis=0, tiled=True)

    def weights_for(normed, routes):
        first, second, onehot = gates(normed, router_w, routes)
        dense = onehot[:, 0, :] * first[:, None] + onehot[:, 1, :] * second[:, None]
        mine = (jnp.arange(experts) == me).astype(jnp.float32)
        return jnp.sum(dense * mine[None, :], axis=1)

    unit_bwd, spread_bwd = normalize(inputs_bwd)
    packed_bwd = unit_bwd.astype(jnp.bfloat16)
    all_bwd = gather(packed_bwd)
    all_up = gather(upstream)
    unit_fwd, _ = normalize(inputs_fwd)
    all_fwd = gather(unit_fwd.astype(jnp.bfloat16))
    routes_bwd = gather(route_bwd[0])
    routes_fwd = gather(route_fwd[0])

    weight = weights_for(all_bwd, routes_bwd)[:, None]
    pre = dot(all_bwd, gate_up_w, 1, 0)
    gate, up = pre[:, :width], pre[:, width:]
    sig = jax.nn.sigmoid(gate)
    active = gate * sig
    hidden = active * up
    up_down = dot(all_up, down_w, 1, 1)
    gate_grad = jnp.sum(hidden * up_down, axis=1, keepdims=True)
    hidden_grad = weight * up_down
    grad_g = hidden_grad * up * sig * (1.0 + gate * (1.0 - sig))
    grad_u = hidden_grad * active
    pre_grad = jnp.concatenate([grad_g, grad_u], axis=1).astype(jnp.bfloat16)
    row_grad = dot(pre_grad, gate_up_w, 1, 1).astype(jnp.bfloat16)
    mine = (jnp.arange(128) == me).astype(jnp.float32)[None, :]
    payload = jnp.concatenate([row_grad, (gate_grad * mine).astype(jnp.bfloat16)], axis=1)
    back = lax.psum_scatter(payload, "expert", scatter_dimension=0, tiled=True)
    gate_up_part = dot(all_bwd, pre_grad, 0, 0).astype(jnp.bfloat16)
    down_part = dot((weight * hidden).astype(jnp.bfloat16), all_up, 0, 0).astype(jnp.bfloat16)
    grad_gate_up = lax.psum_scatter(gate_up_part, "dp", scatter_dimension=0, tiled=True)
    grad_down = lax.psum_scatter(down_part, "dp", scatter_dimension=1, tiled=True)

    weight_f = weights_for(all_fwd, routes_fwd)[:, None]
    pre_f = dot(all_fwd, gate_up_w, 1, 0)
    gate_f, up_f = pre_f[:, :width], pre_f[:, width:]
    hidden_f = (gate_f * jax.nn.sigmoid(gate_f) * up_f).astype(jnp.bfloat16)
    y = (weight_f * dot(hidden_f, down_w, 1, 0)).astype(jnp.bfloat16)
    y_sum = lax.psum_scatter(y, "expert", scatter_dimension=0, tiled=True)
    section_out = (inputs_fwd.astype(jnp.float32) + y_sum.astype(jnp.float32)).astype(jnp.bfloat16)

    first, second, onehot = gates(packed_bwd, router_w, route_bwd[0])
    back_gate = back[:, model : model + experts].astype(jnp.float32)
    pair = onehot[:, 0, :] - onehot[:, 1, :]
    step = first * second * jnp.sum(pair * back_gate, axis=1)
    logit_grad = pair * step[:, None]
    normed_grad = back[:, :model].astype(jnp.float32) + lax.dot_general(
        logit_grad, router_w.astype(jnp.float32), (((1,), (1,)), ((), ())),
        precision=lax.Precision.HIGHEST,
    )
    router_part = lax.dot_general(
        logit_grad, packed_bwd.astype(jnp.float32), (((0,), (0,)), ((), ())),
        precision=lax.Precision.HIGHEST,
    )
    inner = jnp.mean(normed_grad * unit_bwd, axis=1, keepdims=True)
    grad_value = upstream.astype(jnp.float32) + (normed_grad - unit_bwd * inner) / spread_bwd
    input_grad = grad_value.astype(jnp.bfloat16)
    grad_router = lax.psum_scatter(router_part, ("dp", "expert"), scatter_dimension=1, tiled=True).T
    return (
        section_out[None],
        input_grad[None],
        grad_gate_up[None, None],
        grad_down[None, None],
        grad_router[None],
    )


def solution(mesh):
    tokens = P(("dp", "expert"), None)
    sectioned = P("pipe", ("dp", "expert"), None)
    return jax.shard_map(
        shards,
        mesh=mesh,
        in_specs=(
            tokens, tokens, sectioned, sectioned, sectioned, sectioned, sectioned,
            P("pipe", None, None),
            P("pipe", "expert", None, None),
            P("pipe", "expert", None, None),
        ),
        out_specs=(
            sectioned,
            sectioned,
            P("pipe", "expert", "dp", None),
            P("pipe", "expert", None, "dp"),
            sectioned,
        ),
        check_vma=False,
    )
```

time: 334 us -> 322 us (0.964)
  starting transfers between devices: 35.1 us -> 7.62 us
  waiting for transfers between devices: 215 us -> 233 us
  matrix products: 52.5 us -> 35.5 us
  blocking collectives: 0 us -> 12.4 us
  other arithmetic: 9.43 us -> 15.6 us
  local copies, waits for them, and re-layouts: 6.67 us -> 2.96 us
    all_to_all x6 -> x0, waiting for transfers between devices: 151 us -> none  [the longest x2 80.8 us: trade_pair(): lax.all_to_all(rows_part, ('dp', 'expert'), split_axis=0, concat_axis=0,...]
    reduce_scatter x2 -> x4, waiting for transfers between devices: 27.1 us -> 130 us  [the longest x1 46.2 us: shards(): lax.psum_scatter(gate_up_part, 'dp', scatter_dimension=0, tiled=True)]
    unnamed x4 -> x9, waiting for transfers between devices: 0.05 us -> 43.2 us
    all_to_all x6 -> x0, starting transfers between devices: 29.1 us -> none  [the longest x2 11.7 us: trade_pair(): lax.all_to_all(rows_part, ('dp', 'expert'), split_axis=0, concat_axis=0,...]
    all_gather x0 -> x3, waiting for transfers between devices: none -> 23.9 us  [gather(): return lax.all_gather(x, 'expert', axis=0, tiled=True)]
    dot_general x20 -> x11, matrix products: 47.8 us -> 30.9 us  [the longest x7 20.9 us: dot(): lax.dot_general(a, b, (((ca,), (cb,)), ((), ())), preferred_element_type=...]
    all_gather x0 -> x2, blocking collectives: none -> 12.4 us  [gather(): return lax.all_gather(x, 'expert', axis=0, tiled=True)]
  transfers between devices with their start and end apart: 11 -> 10, of which waited for: 8 -> 8; matrix products, arithmetic and copies ran while one was open for 15% -> 13% of each run, Pallas kernels for 0% -> 0%
where the time goes in v1:
time: 322 us
  waiting for transfers between devices  233 us (72%)
  matrix products  35.5 us (11%)
  other arithmetic  15.6 us (5%)
  between operations  14.4 us (4%)
  blocking collectives  12.4 us (4%)
  starting transfers between devices  7.62 us (2%)
    reduce_scatter x1, waiting for transfers between devices, shards(): lax.psum_scatter(gate_up_part, 'dp', scatter_dimension=0, tiled=True)  46.2 us
    unnamed x9, waiting for transfers between devices  43.2 us
    ppermute x2, waiting for transfers between devices, passed_along(): return lax.ppermute(x, axis, pairs)  36.3 us
    reduce_scatter x1, waiting for transfers between devices, shards(): back = lax.psum_scatter(payload, 'expert', scatter_dimension=0, tiled=True)  31 us
    reduce_scatter x1, waiting for transfers between devices, shards(): lax.psum_scatter(down_part, 'dp', scatter_dimension=1, tiled=True)  27.2 us
    reduce_scatter x1, waiting for transfers between devices, shards(): y_sum = lax.psum_scatter(y, 'expert', scatter_dimension=0, tiled=True)  25.6 us
    all_gather x3, waiting for transfers between devices, gather(): return lax.all_gather(x, 'expert', axis=0, tiled=True)  23.9 us
    dot_general x7, matrix products, dot(): lax.dot_general(a, b, (((ca,), (cb,)), ((), ())), preferred_element_type=...  20.9 us
  transfers between devices with their start and end apart: 10, of which 8 were waited for; matrix products, arithmetic and copies ran while one was open for 13% of the time, Pallas kernels for 0%

profile of v1, /device:TPU:0, one launch (start us, length us, event | category | flops | bytes accessed | tf_op | source)
XLA Modules:
  0.0 321.9 jit_solution(5262872061137896950)
XLA Ops:
  7.2 1.5 fusion.8
  8.8 2.2 fusion.57
  11.1 5.8 %collective-permute-start = (bf16[64,6144]{1,0:T(8,128)(2,1)}, bf16[64,6144]{1,0:T(8,128)(2,1)}, u32[]{:S(2)}, u32[]{:S(2)}) collective-permute-start(bf16[64,6144]{1,0:T(8,128)(2,1)} %bitcast.131), channel_id=1, source_target_pairs={{0,4},{4,8},{8,12},{1,5},{5,9},{9,13},{2,6},{6,10},{10,14},{3,7},{... | collective-permute-start | bytes 2359304 | tf_op jit(solution)/shard_map/ppermute | solution.py:12
  16.9 16.2 %collective-permute-done = bf16[64,6144]{1,0:T(8,128)(2,1)} collective-permute-done((bf16[64,6144]{1,0:T(8,128)(2,1)}, bf16[64,6144]{1,0:T(8,128)(2,1)}, u32[]{:S(2)}, u32[]{:S(2)}) %collective-permute-start) | collective-permute-done | bytes 786464 | tf_op jit(solution)/shard_map/ppermute | solution.py:12
  33.1 1.5 fusion.10
  35.5 1.1 fusion.11
  36.7 1.3 collective-permute-start.1
  38.0 20.1 %collective-permute-done.1 = bf16[64,6144]{1,0:T(8,128)(2,1)} collective-permute-done((bf16[64,6144]{1,0:T(8,128)(2,1)}, bf16[64,6144]{1,0:T(8,128)(2,1)}, u32[]{:S(2)}, u32[]{:S(2)}) %collective-permute-start.1) | collective-permute-done | bytes 786464 | tf_op jit(solution)/shard_map/ppermute | solution.py:12
  58.1 2.1 broadcast_select_fusion
  60.5 6.2 %all-gather.1 = s32[1,256,2]{2,0,1:T(1,128)S(1)} all-gather(s32[1,64,2]{2,0,1:T(1,128)S(1)} %copy.50), channel_id=3, replica_groups=mesh['dp'=2,'pipe'=4,'expert'=4] {'expert'}, dimensions={1}, use_global_device_ids=true | all-gather | bytes 2560 | tf_op jit(solution)/shard_map/all_gather | solution.py:54
  66.7 6.2 %all-gather = s32[1,256,2]{2,0,1:T(1,128)S(1)} all-gather(s32[1,64,2]{2,0,1:T(1,128)S(1)} %copy.48), channel_id=2, replica_groups=mesh['dp'=2,'pipe'=4,'expert'=4] {'expert'}, dimensions={1}, use_global_device_ids=true | all-gather | bytes 2560 | tf_op jit(solution)/shard_map/all_gather | solution.py:54
  73.1 3.0 fusion.28
  76.2 1.7 fusion.2
  77.9 2.8 fusion.30
  80.8 23.9 %all-gather.10.cloned.1.call-done = bf16[256,6144]{1,0:T(8,128)(2,1)} async-done(((bf16[64,6144]{1,0:T(8,128)(2,1)}), bf16[256,6144]{1,0:T(8,128)(2,1)}) %all-gather.10.cloned.1.call-update) | async-done | bytes 3145744 | tf_op jit(solution)/shard_map/all_gather | solution.py:54
  104.8 3.4 %multiply_convert_fusion.3 = (bf16[256,128]{1,0:T(8,128)(2,1)S(1)}, bf16[256,128]{1,0:T(8,128)(2,1)S(1)}, f32[256]{0:T(256)S(1)}) fusion(f32[256,256]{1,0:T(8,128)} %fusion.2, f32[256]{0:T(256)S(1)} %get-tuple-element.5, bf16[256,6144]{1,0:T(8,128)(2,1)} %all-gather.10.cloned.1.call-done, bf16[1,1,128,6144]{3,2,1,0:T(8,128)(2,1)} %param.19), kind=kOutput, calls=%fused_computation.42 | convolution fusion | flops 403209984 | bytes 5113856 | tf_op jit(solution)/shard_map/dot_general | solution.py:16
  109.3 1.9 pad_maximum_fusion
  111.4 3.0 fusion.4
  114.4 2.6 fusion
  117.0 1.6 fusion.26
  118.9 31.0 %reduce-scatter.10.cloned.1.call-done = bf16[64,6272]{1,0:T(8,128)(2,1)} async-done(((bf16[256,6272]{1,0:T(8,128)(2,1)}), bf16[64,6272]{1,0:T(8,128)(2,1)}) %reduce-scatter.10.cloned.1.call-update) | async-done | bytes 802832 | tf_op jit(solution)/shard_map/reduce_scatter | solution.py:86
  150.7 4.6 %convolution_bitcast_fusion = f32[6144,4]{1,0:T(8,128)} fusion(f32[64]{0:T(128)S(1)} %fusion.52, f32[64,2,4]{2,0,1:T(8,128)S(1)} %fusion.22, bf16[1,64,6144]{2,1,0:T(8,128)(2,1)} %param.14, f32[64]{0:T(128)S(1)} %add_sqrt_fusion), kind=kOutput, calls=%fused_computation.4 | convolution fusion | flops 20054528 | bytes 887296
  155.4 3.9 %convolution_convert_fusion.2 = bf16[128,6144]{1,0:T(8,128)(2,1)} fusion(bf16[256,6144]{1,0:T(8,128)(2,1)} %all-gather.10.cloned.1.call-done, f32[256]{0:T(256)S(1)} %get-tuple-element.5, f32[256,256]{1,0:T(8,128)} %fusion.2), kind=kOutput, calls=%fused_computation.5 | convolution fusion | flops 403668992 | bytes 4981760 | tf_op jit(solution)/shard_map/dot_general | solution.py:16
  159.6 5.2 %convolution_convert_fusion = bf16[6144,256]{1,0:T(8,128)(2,1)} fusion(bf16[256,6144]{1,0:T(8,128)(2,1)} %all-gather.8.cloned.1.call-done, bf16[256,128]{1,0:T(8,128)(2,1)S(1)} %get-tuple-element.10, bf16[256,128]{1,0:T(8,128)(2,1)S(1)} %get-tuple-element.9), kind=kOutput, calls=%fused_computation.2 | convolution fusion | flops 807141376 | bytes 6422528 | tf_op jit(solution)/shard_map/dot_general | solution.py:16
  164.8 25.6 %reduce-scatter.8.cloned.1.call-done = bf16[64,6144]{1,0:T(8,128)(2,1)} async-done(((bf16[256,6144]{1,0:T(8,128)(2,1)}), bf16[64,6144]{1,0:T(8,128)(2,1)}) %reduce-scatter.8.cloned.1.call-update) | async-done | bytes 786448 | tf_op jit(solution)/shard_map/reduce_scatter | solution.py:97
  190.4 2.4 fusion.16
  192.8 2.6 multiply_reduce_fusion
  195.5 1.3 fusion.18
  196.8 43.1 %reduce-scatter.16.cloned.1.call-done = f32[768,4]{1,0:T(8,128)} async-done(((f32[6144,4]{1,0:T(8,128)}), f32[768,4]{1,0:T(8,128)}) %reduce-scatter.16.cloned.1.call-update) | async-done | bytes 12304
  239.9 1.7 copy.61
  241.7 27.2 %reduce-scatter.14.cloned.1.call-done = bf16[128,3072]{1,0:T(8,128)(2,1)} async-done(((bf16[128,6144]{1,0:T(8,128)(2,1)}), bf16[128,3072]{1,0:T(8,128)(2,1)}) %reduce-scatter.14.cloned.1.call-update) | async-done | bytes 786448 | tf_op jit(solution)/shard_map/reduce_scatter | solution.py:90
  268.9 46.2 %reduce-scatter.12.cloned.1.call-done = bf16[3072,256]{1,0:T(8,128)(2,1)} async-done(((bf16[6144,256]{1,0:T(8,128)(2,1)}), bf16[3072,256]{1,0:T(8,128)(2,1)}) %reduce-scatter.12.cloned.1.call-update) | async-done | bytes 1572880 | tf_op jit(solution)/shard_map/reduce_scatter | solution.py:89
  (57 shorter events, 4.3 us)
Async XLA Ops:
  7.2 69.0 %copy-start = (bf16[1,1,6144,256]{3,2,1,0:T(8,128)(2,1)S(1)}, bf16[1,1,6144,256]{3,2,1,0:T(8,128)(2,1)}, u32[]{:S(2)}) copy-start(bf16[1,1,6144,256]{3,2,1,0:T(8,128)(2,1)} %param.18) | copy-start | bytes 9437188
  7.2 65.9 %all-gather.8.cloned.1.call-start = ((), (), s32[]{:S(2)}) async-start(), calls=%async_computation.7 | async-start | bytes 3932160 | tf_op jit(solution)/shard_map/all_gather | solution.py:54
  11.0 66.9 %all-gather.6.cloned.1.call-start = ((), (), s32[]{:S(2)}) async-start(), calls=%async_computation.5 | async-start | bytes 3932160 | tf_op jit(solution)/shard_map/all_gather | solution.py:54
  11.1 22.0 %collective-permute-start = (bf16[64,6144]{1,0:T(8,128)(2,1)}, bf16[64,6144]{1,0:T(8,128)(2,1)}, u32[]{:S(2)}, u32[]{:S(2)}) collective-permute-start(bf16[64,6144]{1,0:T(8,128)(2,1)} %bitcast.131), channel_id=1, source_target_pairs={{0,4},{4,8},{8,12},{1,5},{5,9},{9,13},{2,6},{6,10},{10,14},{3,7},{... | collective-permute-start | bytes 2359304 | tf_op jit(solution)/shard_map/ppermute | solution.py:12
  34.7 0.9 copy-start.4
  34.7 25.6 %copy-start.8 = (s32[1,64,2]{1,2,0:T(2,128)S(1)}, s32[1,64,2]{1,2,0:T(2,128)}, u32[]{:S(2)}) copy-start(s32[1,64,2]{1,2,0:T(2,128)} %param.15) | copy-start | bytes 1540
  34.7 25.7 %copy-start.7 = (s32[1,64,2]{1,2,0:T(2,128)S(1)}, s32[1,64,2]{1,2,0:T(2,128)}, u32[]{:S(2)}) copy-start(s32[1,64,2]{1,2,0:T(2,128)} %param.16) | copy-start | bytes 1540
  34.7 38.4 %copy-start.6 = (bf16[1,6144,4]{1,2,0:T(4,128)(2,1)S(1)}, bf16[1,6144,4]{1,2,0:T(4,128)(2,1)}, u32[]{:S(2)}) copy-start(bf16[1,6144,4]{1,2,0:T(4,128)(2,1)} %param.17) | copy-start | bytes 147460
  36.7 68.1 %all-gather.10.cloned.1.call-start = ((), (), s32[]{:S(2)}) async-start(), calls=%async_computation.8 | async-start | bytes 3932160 | tf_op jit(solution)/shard_map/all_gather | solution.py:54
  36.7 21.4 %collective-permute-start.1 = (bf16[64,6144]{1,0:T(8,128)(2,1)}, bf16[64,6144]{1,0:T(8,128)(2,1)}, u32[]{:S(2)}, u32[]{:S(2)}) collective-permute-start(bf16[64,6144]{1,0:T(8,128)(2,1)} %bitcast.132), channel_id=1, source_target_pairs={{4,0},{8,4},{12,8},{5,1},{9,5},{13,9},{6,2},{10,6},{14,10},{7,3},{... | collective-permute-start | bytes 2359304 | tf_op jit(solution)/shard_map/ppermute | solution.py:12
  60.2 89.6 %reduce-scatter.10.cloned.1.call-start = ((), (), s32[]{:S(2)}) async-start(), calls=%async_computation.9 | async-start | bytes 4014080 | tf_op jit(solution)/shard_map/reduce_scatter | solution.py:86
  73.1 3.1 copy-start.1
  111.3 79.1 %reduce-scatter.8.cloned.1.call-start = ((), (), s32[]{:S(2)}) async-start(), calls=%async_computation.6 | async-start | bytes 3932160 | tf_op jit(solution)/shard_map/reduce_scatter | solution.py:97
  111.3 3.0 copy-start.5
  117.0 122.9 %reduce-scatter.16.cloned.1.call-start = ((), (), s32[]{:S(2)}) async-start(), calls=%async_computation.12 | async-start | bytes 3538944
  155.3 113.6 %reduce-scatter.14.cloned.1.call-start = ((), (), s32[]{:S(2)}) async-start(), calls=%async_computation.11 | async-start | bytes 2359296 | tf_op jit(solution)/shard_map/reduce_scatter | solution.py:90
  159.3 155.7 %reduce-scatter.12.cloned.1.call-start = ((), (), s32[]{:S(2)}) async-start(), calls=%async_computation.10 | async-start | bytes 4718592 | tf_op jit(solution)/shard_map/reduce_scatter | solution.py:89
  192.8 2.7 copy-start.2
  192.8 2.7 copy-start.3
Sparse Core Ops, SparseCore 0:
  11.2 31.2 all-gather.7
  44.6 29.9 all-gather.5
  76.1 28.6 all-gather.9
  111.4 38.3 reduce-scatter.9
  152.4 37.9 reduce-scatter.7
  193.6 46.2 reduce-scatter.15
  242.8 26.0 reduce-scatter.13
  271.7 43.3 reduce-scatter.11

commit v2 on v1

v2 whole, which is shorter than its diff:
```python
import functools

import jax
import jax.numpy as jnp
from jax import lax
from jax.experimental import pallas as pl
from jax.experimental.pallas import tpu as pltpu
from jax.sharding import PartitionSpec as P

EPSILON = 1e-05
MESH = pl.DeviceIdType.MESH
IDS = 16
STRIP = 16


def dot(a, b, ca, cb, precision=None):
    return lax.dot_general(
        a, b, (((ca,), (cb,)), ((), ())), precision=precision, preferred_element_type=jnp.float32
    )


class Gather:
    def __init__(self, view, send, recv, chips, x, c):
        self.view, self.send, self.recv = view, send, recv
        self.chips, self.x, self.c = chips, x, c

    def copy(self, block, at, target):
        ref = self.view(block)
        return pltpu.make_async_remote_copy(
            src_ref=ref, dst_ref=ref, send_sem=self.send.at[at], recv_sem=self.recv.at[at],
            device_id={"expert": target}, device_id_type=MESH,
        )

    def here(self, i, core):
        return lax.rem(self.x + self.chips - i, self.chips) * 2 + core

    def start(self):
        own = self.x * 2 + self.c
        for i in range(1, self.chips):
            self.copy(own, i, lax.rem(self.x + i, self.chips) * 2 + self.c).start()
        self.copy(own, 0, self.x * 2 + 1 - self.c).start()

    def forward(self):
        other = self.x * 2 + 1 - self.c
        for i in range(1, self.chips):
            self.copy(self.here(i, self.c), i, other).wait_recv()
            self.copy(self.here(i, self.c), self.chips - 1 + i, other).start()

    def finish(self):
        other = self.x * 2 + 1 - self.c
        self.copy(other, 0, other).wait_recv()
        for i in range(1, self.chips):
            self.copy(self.here(i, 1 - self.c), self.chips - 1 + i, other).wait_recv()

    def sent(self):
        other = self.x * 2 + 1 - self.c
        own = self.x * 2 + self.c
        self.copy(own, 0, other).wait_send()
        for i in range(1, self.chips):
            self.copy(own, i, other).wait_send()
            self.copy(self.here(i, self.c), self.chips - 1 + i, other).wait_send()


class Scatter:
    def __init__(self, view, pair, cross, sems, chips, x, c):
        self.view, self.pair, self.cross = view, pair, cross
        self.pair_send, self.pair_recv, self.cross_send, self.cross_recv = sems
        self.chips, self.x, self.c = chips, x, c

    def pair_copy(self, i):
        to = lax.rem(self.x + i, self.chips) * 2 + 1 - self.c
        return pltpu.make_async_remote_copy(
            src_ref=self.view(to), dst_ref=self.pair.at[i],
            send_sem=self.pair_send.at[i], recv_sem=self.pair_recv.at[i],
            device_id={"expert": self.x * 2 + 1 - self.c}, device_id_type=MESH,
        )

    def cross_copy(self, i):
        return pltpu.make_async_remote_copy(
            src_ref=self.pair.at[i], dst_ref=self.cross.at[i - 1],
            send_sem=self.cross_send.at[i - 1], recv_sem=self.cross_recv.at[i - 1],
            device_id={"expert": lax.rem(self.x + i, self.chips) * 2 + self.c}, device_id_type=MESH,
        )

    def order(self):
        return list(range(1, self.chips)) + [0]

    def start(self):
        for i in self.order():
            self.pair_copy(i).start()

    def forward(self):
        for i in range(1, self.chips):
            self.pair_copy(i).wait_recv()
            mine = self.view(lax.rem(self.x + i, self.chips) * 2 + self.c)

            def add(k, carry, i=i, mine=mine):
                rows = pl.ds(pl.multiple_of(k * STRIP, STRIP), STRIP)
                self.pair[i, rows, :] = (
                    self.pair[i, rows, :].astype(jnp.float32) + mine[rows, :].astype(jnp.float32)
                ).astype(jnp.bfloat16)
                return carry

            lax.fori_loop(0, self.pair.shape[1] // STRIP, add, 0)
            self.cross_copy(i).start()

    def finish(self):
        self.pair_copy(0).wait_recv()
        for i in range(1, self.chips):
            self.cross_copy(i).wait_recv()

    def total(self, rows):
        value = self.view(self.x * 2 + self.c)[rows, :].astype(jnp.float32)
        value = value + self.pair[0, rows, :].astype(jnp.float32)
        for i in range(1, self.chips):
            value = value + self.cross[i - 1, rows, :].astype(jnp.float32)
        return value

    def sent(self):
        for i in range(self.chips):
            self.pair_copy(i).wait_send()
        for i in range(1, self.chips):
            self.cross_copy(i).wait_send()


def kernel(
    dims,
    fresh, cotangent, prev_out, prev_grad, saved_in, lanes_fwd, lanes_bwd, router_b, router_f,
    gate_up, down,
    section_out, input_grad, grad_gate_up, grad_down, grad_router,
    all_bwd, all_fwd, all_up, part, pair_row, cross_row, pair_y, cross_y,
    gate_up_w, down_w, saved, inputs_fwd, gu_send, gu_recv, dn_send, dn_recv, rt_send, rt_recv,
    gates_all, pre_acc, log_acc, hid_acc, grad_pre, hid_weighted, logit_ref, rt_own,
    local_sem, pipe_send, pipe_recv, g_send, g_recv, s_psend, s_precv, s_csend, s_crecv,
    gu_ss, gu_rs, dn_ss, dn_rs, rt_ss, rt_rs,
):
    sections, replicas, owners = dims
    tokens, model = saved.shape
    width = down_w.shape[0]
    experts = owners
    chips = owners // 2
    total = owners * tokens
    piece = model // replicas
    chunk = gu_send.shape[2]
    steps = gu_send.shape[1]
    rt_width = rt_own.shape[1]
    rt_step = rt_width if rt_width < piece else 0

    section = lax.axis_index("pipe")
    dp = lax.axis_index("dp")
    me = lax.axis_index("expert")
    x, c = me // 2, lax.rem(me, 2)
    has_prev = section > 0
    has_next = section < sections - 1
    own_rows = pl.ds(pl.multiple_of(me * tokens, tokens), tokens)

    load_saved = pltpu.make_async_copy(saved_in, saved, local_sem.at[0])
    load_gate = pltpu.make_async_copy(gate_up, gate_up_w, local_sem.at[1])
    load_down = pltpu.make_async_copy(down, down_w, local_sem.at[2])
    load_fresh = pltpu.make_async_copy(fresh, inputs_fwd, local_sem.at[3])
    load_cot = pltpu.make_async_copy(cotangent, all_up.at[own_rows], local_sem.at[4])
    load_saved.start()
    load_gate.start()
    load_down.start()

    barrier = pltpu.get_barrier_semaphore()

    @pl.when(has_prev)
    def _():
        pl.semaphore_signal(barrier, inc=1, device_id={"pipe": section - 1}, device_id_type=MESH)

    @pl.when(has_next)
    def _():
        pl.semaphore_signal(barrier, inc=1, device_id={"pipe": section + 1}, device_id_type=MESH)

    pl.semaphore_signal(barrier, inc=1, device_id={"expert": x * 2 + 1 - c}, device_id_type=MESH)
    for i in range(1, chips):
        pl.semaphore_signal(
            barrier, inc=1, device_id={"expert": lax.rem(x + i, chips) * 2 + c}, device_id_type=MESH
        )
    for i in range(1, replicas):
        pl.semaphore_signal(
            barrier, inc=1, device_id={"dp": lax.rem(dp + i, replicas)}, device_id_type=MESH
        )

    def strips(body):
        def step(k, carry):
            body(pl.multiple_of(k * STRIP, STRIP))
            return carry

        lax.fori_loop(0, tokens // STRIP, step, 0)

    def inverse(values):
        return 1.0 / jnp.sqrt(jnp.mean(values * values, axis=1, keepdims=True) + EPSILON)

    def normalize_into(source, target, lanes):
        def body(at):
            values = source[pl.ds(at, STRIP), :].astype(jnp.float32)
            rows = pl.ds(pl.multiple_of(me * tokens + at, STRIP), STRIP)
            target[rows, :model] = (values * inverse(values)).astype(jnp.bfloat16)
            target[rows, model:] = lanes[pl.ds(at, STRIP), :]

        strips(body)

    load_saved.wait()
    normalize_into(saved, all_bwd, lanes_bwd)
    pl.semaphore_wait(
        barrier,
        chips + replicas - 1 + jnp.minimum(section, 1) + jnp.minimum(sections - 1 - section, 1),
    )

    send_out = pltpu.make_async_remote_copy(
        src_ref=prev_out, dst_ref=inputs_fwd, send_sem=pipe_send.at[0], recv_sem=pipe_recv.at[0],
        device_id={"pipe": lax.rem(section + 1, sections)}, device_id_type=MESH,
    )
    send_grad = pltpu.make_async_remote_copy(
        src_ref=prev_grad, dst_ref=all_up.at[own_rows],
        send_sem=pipe_send.at[1], recv_sem=pipe_recv.at[1],
        device_id={"pipe": lax.rem(section + sections - 1, sections)}, device_id_type=MESH,
    )

    @pl.when(has_prev)
    def _():
        send_grad.start()

    @pl.when(has_next)
    def _():
        send_out.start()

    @pl.when(jnp.logical_not(has_prev))
    def _():
        load_fresh.start()

    @pl.when(jnp.logical_not(has_next))
    def _():
        load_cot.start()

    def block_of(ref):
        return lambda j: ref.at[pl.ds(pl.multiple_of(j * tokens, tokens), tokens)]

    gather_bwd = Gather(block_of(all_bwd), g_send.at[0], g_recv.at[0], chips, x, c)
    gather_up = Gather(block_of(all_up), g_send.at[1], g_recv.at[1], chips, x, c)
    gather_fwd = Gather(block_of(all_fwd), g_send.at[2], g_recv.at[2], chips, x, c)
    gather_gate = Gather(lambda j: gates_all.at[j], g_send.at[3], g_recv.at[3], chips, x, c)
    sems = [
        tuple(ref.at[a] for ref in (s_psend, s_precv, s_csend, s_crecv)) for a in range(2)
    ]
    scatter_row = Scatter(block_of(part), pair_row, cross_row, sems[0], chips, x, c)

    def narrow(j):
        return all_bwd.at[pl.ds(pl.multiple_of(j * tokens, tokens), tokens), pl.ds(0, model)]

    scatter_y = Scatter(narrow, pair_y, cross_y, sems[1], chips, x, c)

    def columns(k):
        return pl.ds(pl.multiple_of(k * chunk, chunk), chunk)

    def chunks(body):
        def step(k, carry):
            body(columns(k))
            return carry

        lax.fori_loop(0, model // chunk, step, 0)

    lane = lax.broadcasted_iota(jnp.int32, (total, IDS), 1).astype(jnp.float32)
    mine = (lane == me.astype(jnp.float32)).astype(jnp.float32)

    def project(rows_ref):
        pre_acc[...] = jnp.zeros_like(pre_acc)
        log_acc[...] = jnp.zeros_like(log_acc)

        def body(cols):
            rows = rows_ref[:, cols]
            pre_acc[...] += dot(rows, gate_up_w[cols, :], 1, 0)
            log_acc[...] += dot(rows, router_b[:, cols], 1, 1)

        chunks(body)
        ids = rows_ref[:, model:].astype(jnp.float32)
        one = (lane == ids[:, 0:1]).astype(jnp.float32)
        two = (lane == ids[:, 1:2]).astype(jnp.float32)
        logits = log_acc[...]
        apart = jnp.sum((one - two) * logits, axis=1, keepdims=True)
        first, second = jax.nn.sigmoid(apart), jax.nn.sigmoid(-apart)
        weight = jnp.sum((one * first + two * second) * mine, axis=1, keepdims=True)
        return one, two, first, second, weight, pre_acc[:, :width], pre_acc[:, width:]

    gather_bwd.start()

    @pl.when(has_next)
    def _():
        send_grad.wait_recv()

    @pl.when(jnp.logical_not(has_next))
    def _():
        load_cot.wait()

    gather_up.start()
    gather_bwd.forward()

    @pl.when(has_prev)
    def _():
        send_out.wait_recv()

    @pl.when(jnp.logical_not(has_prev))
    def _():
        load_fresh.wait()

    normalize_into(inputs_fwd, all_fwd, lanes_fwd)
    load_gate.wait()
    load_down.wait()
    gather_bwd.finish()
    one, two, first, second, weight, gate, up = project(all_bwd)
    sig = jax.nn.sigmoid(gate)
    active = gate * sig
    hidden = active * up
    hid_weighted[...] = (weight * hidden).astype(jnp.bfloat16)

    gather_up.forward()
    gather_fwd.start()
    gather_up.finish()
    hid_acc[...] = jnp.zeros_like(hid_acc)

    def up_body(cols):
        hid_acc[...] += dot(all_up[:, cols], down_w[:, cols], 1, 1)

    chunks(up_body)
    up_down = hid_acc[...]
    gate_grad = jnp.sum(hidden * up_down, axis=1, keepdims=True)
    lanes = lax.broadcasted_iota(jnp.int32, (total, 128), 1).astype(jnp.float32)
    gates_all[me] = (gate_grad * (lanes == me.astype(jnp.float32)).astype(jnp.float32)).astype(
        jnp.bfloat16
    )
    gather_gate.start()
    hidden_grad = weight * up_down
    grad_pre[:, :width] = (hidden_grad * up * sig * (1.0 + gate * (1.0 - sig))).astype(jnp.bfloat16)
    grad_pre[:, width:] = (hidden_grad * active).astype(jnp.bfloat16)

    def gu_copy(i, k):
        return pltpu.make_async_remote_copy(
            src_ref=gu_send.at[i - 1, k], dst_ref=gu_recv.at[i - 1, k],
            send_sem=gu_ss.at[i - 1, k], recv_sem=gu_rs.at[i - 1, k],
            device_id={"dp": lax.rem(dp + i, replicas)}, device_id_type=MESH,
        )

    def dn_copy(i, k):
        return pltpu.make_async_remote_copy(
            src_ref=dn_send.at[i - 1, k], dst_ref=dn_recv.at[i - 1, k],
            send_sem=dn_ss.at[i - 1, k], recv_sem=dn_rs.at[i - 1, k],
            device_id={"dp": lax.rem(dp + i, replicas)}, device_id_type=MESH,
        )

    def weight_parts(owner, k):
        cols = pl.ds(pl.multiple_of(owner * piece + k * chunk, chunk), chunk)
        gu = dot(all_bwd[:, cols], grad_pre[...], 0, 0).astype(jnp.bfloat16)
        dn = dot(hid_weighted[...], all_up[:, cols], 0, 0).astype(jnp.bfloat16)
        return gu, dn

    for i in range(1, replicas):
        def send_step(k, carry, i=i):
            gu, dn = weight_parts(lax.rem(dp + i, replicas), k)
            gu_send[i - 1, k] = gu
            dn_send[i - 1, k] = dn
            gu_copy(i, k).start()
            dn_copy(i, k).start()
            return carry

        lax.fori_loop(0, steps, send_step, 0)

    def row_body(cols):
        part[:, cols] = dot(grad_pre[...], gate_up_w[cols, :], 1, 1).astype(jnp.bfloat16)

    chunks(row_body)
    scatter_row.start()

    def own_step(k, carry):
        gu, dn = weight_parts(dp, k)
        grad_gate_up[columns(k), :] = gu
        grad_down[:, columns(k)] = dn
        return carry

    gather_gate.forward()
    scatter_row.forward()
    lax.fori_loop(0, steps, own_step, 0)

    gather_gate.finish()
    gate_all = gates_all[0].astype(jnp.float32)
    for j in range(1, owners):
        gate_all = gate_all + gates_all[j].astype(jnp.float32)
    logit = (one - two) * (
        first * second * jnp.sum((one - two) * gate_all[:, :IDS], axis=1, keepdims=True)
    )
    logit_ref[...] = logit

    def rt_copy(i):
        return pltpu.make_async_remote_copy(
            src_ref=rt_send.at[i - 1], dst_ref=rt_recv.at[i - 1],
            send_sem=rt_ss.at[i - 1], recv_sem=rt_rs.at[i - 1],
            device_id={"dp": lax.rem(dp + i, replicas)}, device_id_type=MESH,
        )

    def router_part(owner):
        cols = pl.ds(pl.multiple_of(owner * piece + me * rt_step, 128), rt_width)
        return dot(
            logit_ref[...], all_bwd[:, cols].astype(jnp.float32), 0, 0, lax.Precision.HIGHEST
        )

    for i in range(1, replicas):
        rt_send[i - 1] = router_part(lax.rem(dp + i, replicas))
        rt_copy(i).start()
    rt_own[...] = router_part(dp)

    gather_fwd.forward()
    gather_fwd.finish()
    gather_bwd.sent()
    _, _, _, _, weight_f, gate_f, up_f = project(all_fwd)
    hid_weighted[...] = (weight_f * (gate_f * jax.nn.sigmoid(gate_f) * up_f)).astype(jnp.bfloat16)

    def y_body(cols):
        all_bwd[:, cols] = dot(hid_weighted[...], down_w[:, cols], 1, 0).astype(jnp.bfloat16)

    chunks(y_body)
    scatter_y.start()
    scatter_y.forward()

    scatter_row.finish()

    def grad_body(at):
        rows = pl.ds(at, STRIP)
        home = pl.ds(pl.multiple_of(me * tokens + at, STRIP), STRIP)
        values = saved[rows, :].astype(jnp.float32)
        inv = inverse(values)
        unit = values * inv
        normed_grad = scatter_row.total(rows)
        steps_here = logit_ref[home, :]
        for j in range(experts):
            normed_grad = normed_grad + steps_here[:, j : j + 1] * router_f[j : j + 1, :]
        inner = jnp.mean(normed_grad * unit, axis=1, keepdims=True)
        input_grad[rows, :] = (
            all_up[home, :].astype(jnp.float32) + (normed_grad - unit * inner) * inv
        ).astype(jnp.bfloat16)

    strips(grad_body)

    rt = rt_own[...]
    for i in range(1, replicas):
        rt_copy(i).wait_recv()
        rt = rt + rt_recv[i - 1]
    grad_router[...] = rt

    for i in range(1, replicas):
        def add_step(k, carry, i=i):
            gu_copy(i, k).wait_recv()
            dn_copy(i, k).wait_recv()
            cols = columns(k)
            grad_gate_up[cols, :] = (
                grad_gate_up[cols, :].astype(jnp.float32) + gu_recv[i - 1, k].astype(jnp.float32)
            ).astype(jnp.bfloat16)
            grad_down[:, cols] = (
                grad_down[:, cols].astype(jnp.float32) + dn_recv[i - 1, k].astype(jnp.float32)
            ).astype(jnp.bfloat16)
            return carry

        lax.fori_loop(0, steps, add_step, 0)

    scatter_y.finish()

    def out_body(at):
        rows = pl.ds(at, STRIP)
        section_out[rows, :] = (
            inputs_fwd[rows, :].astype(jnp.float32) + scatter_y.total(rows)
        ).astype(jnp.bfloat16)

    strips(out_body)

    @pl.when(has_prev)
    def _():
        send_grad.wait_send()

    @pl.when(has_next)
    def _():
        send_out.wait_send()

    gather_up.sent()
    gather_fwd.sent()
    gather_gate.sent()
    scatter_row.sent()
    scatter_y.sent()
    for i in range(1, replicas):
        rt_copy(i).wait_send()

        def drain(k, carry, i=i):
            gu_copy(i, k).wait_send()
            dn_copy(i, k).wait_send()
            return carry

        lax.fori_loop(0, steps, drain, 0)


def shards(
    fresh, cotangent, prev_out, prev_grad, saved_in, route_fwd, route_bwd, router, gate_up, down
):
    sections = lax.axis_size("pipe")
    replicas = lax.axis_size("dp")
    owners = lax.axis_size("expert")
    tokens, model = fresh.shape
    width = down.shape[2]
    experts = router.shape[2]
    chips = owners // 2
    total = owners * tokens
    piece = model // replicas
    chunk = min(768, piece)
    steps = piece // chunk
    rt_width = piece // owners if (piece // owners) % 128 == 0 else piece

    def lanes(routes):
        return jnp.pad(routes[0].astype(jnp.bfloat16), ((0, 0), (0, 126)))

    router_f = jnp.pad(router[0].T.astype(jnp.float32), ((0, IDS - experts), (0, 0)))
    bf16, f32 = jnp.bfloat16, jnp.float32
    far = max(replicas - 1, 1)
    dma = pltpu.SemaphoreType.DMA
    any_spec = pl.BlockSpec(memory_space=pl.ANY)
    vmem = pl.BlockSpec(memory_space=pltpu.VMEM)
    outs = pl.pallas_call(
        functools.partial(kernel, (sections, replicas, owners)),
        out_shape=(
            jax.ShapeDtypeStruct((tokens, model), bf16),
            jax.ShapeDtypeStruct((tokens, model), bf16),
            jax.ShapeDtypeStruct((piece, 2 * width), bf16),
            jax.ShapeDtypeStruct((width, piece), bf16),
            jax.ShapeDtypeStruct((IDS, rt_width), f32),
        ),
        in_specs=[any_spec] * 5 + [vmem] * 4 + [any_spec] * 2,
        out_specs=(vmem,) * 5,
        scratch_shapes=[
            pltpu.VMEM((total, model + 128), bf16),
            pltpu.VMEM((total, model + 128), bf16),
            pltpu.VMEM((total, model), bf16),
            pltpu.VMEM((total, model), bf16),
            pltpu.VMEM((chips, tokens, model), bf16),
            pltpu.VMEM((chips - 1, tokens, model), bf16),
            pltpu.VMEM((chips, tokens, model), bf16),
            pltpu.VMEM((chips - 1, tokens, model), bf16),
            pltpu.VMEM((model, 2 * width), bf16),
            pltpu.VMEM((width, model), bf16),
            pltpu.VMEM((tokens, model), bf16),
            pltpu.VMEM((tokens, model), bf16),
            pltpu.VMEM((far, steps, chunk, 2 * width), bf16),
            pltpu.VMEM((far, steps, chunk, 2 * width), bf16),
            pltpu.VMEM((far, steps, width, chunk), bf16),
            pltpu.VMEM((far, steps, width, chunk), bf16),
            pltpu.VMEM((far, IDS, rt_width), f32),
            pltpu.VMEM((far, IDS, rt_width), f32),
            pltpu.VMEM((owners, total, 128), bf16),
            pltpu.VMEM((total, 2 * width), f32),
            pltpu.VMEM((total, IDS), f32),
            pltpu.VMEM((total, width), f32),
            pltpu.VMEM((total, 2 * width), bf16),
            pltpu.VMEM((total, width), bf16),
            pltpu.VMEM((total, IDS), f32),
            pltpu.VMEM((IDS, rt_width), f32),
            dma((5,)),
            dma((2,)),
            dma((2,)),
            dma((4, 2 * chips - 1)),
            dma((4, 2 * chips - 1)),
            dma((2, chips)),
            dma((2, chips)),
            dma((2, chips - 1)),
            dma((2, chips - 1)),
            dma((far, steps)),
            dma((far, steps)),
            dma((far, steps)),
            dma((far, steps)),
            dma((far,)),
            dma((far,)),
        ],
        compiler_params=pltpu.CompilerParams(
            collective_id=0, has_side_effects=True, vmem_limit_bytes=62 * 2**20
        ),
        name="relay_step",
    )(
        fresh, cotangent, prev_out[0], prev_grad[0], saved_in[0], lanes(route_fwd),
        lanes(route_bwd), router_f.astype(bf16), router_f, gate_up[0, 0], down[0, 0],
    )
    section_out, input_grad, grad_gate_up, grad_down, grad_router = outs
    share = piece // owners
    if rt_width != share:
        grad_router = lax.dynamic_slice_in_dim(
            grad_router, lax.axis_index("expert") * share, share, axis=1
        )
    return (
        section_out[None],
        input_grad[None],
        grad_gate_up[None, None],
        grad_down[None, None],
        grad_router[:experts].T[None],
    )


def solution(mesh):
    tokens = P(("dp", "expert"), None)
    sectioned = P("pipe", ("dp", "expert"), None)
    return jax.shard_map(
        shards,
        mesh=mesh,
        in_specs=(
            tokens, tokens, sectioned, sectioned, sectioned, sectioned, sectioned,
            P("pipe", None, None),
            P("pipe", "expert", None, None),
            P("pipe", "expert", None, None),
        ),
        out_specs=(
            sectioned,
            sectioned,
            P("pipe", "expert", "dp", None),
            P("pipe", "expert", None, "dp"),
            sectioned,
        ),
        check_vma=False,
    )
```

time: 322 us -> 115 us (0.36)
  waiting for transfers between devices: 233 us -> 0 us
  Pallas kernels: 0 us -> 102 us
  matrix products: 35.5 us -> 0 us
  between operations: 14.4 us -> 0.66 us
  other arithmetic: 15.6 us -> 3.01 us
  blocking collectives: 12.4 us -> 0 us
  starting transfers between devices: 7.62 us -> 0 us
  local copies, waits for them, and re-layouts: 2.96 us -> 8.49 us
    reduce_scatter x4 -> x0, waiting for transfers between devices: 130 us -> none  [the longest x1 46.2 us: shards(): lax.psum_scatter(gate_up_part, 'dp', scatter_dimension=0, tiled=True)]
    pallas_call x0 -> x1, Pallas kernels: none -> 102 us  [shards(): pl.pallas_call(functools.partial(kernel, (sections, replicas, owners)), o...]
    unnamed x9 -> x0, waiting for transfers between devices: 43.2 us -> none
    ppermute x2 -> x0, waiting for transfers between devices: 36.3 us -> none  [passed_along(): return lax.ppermute(x, axis, pairs)]
    dot_general x11 -> x0, matrix products: 30.9 us -> none  [the longest x7 20.9 us: dot(): lax.dot_general(a, b, (((ca,), (cb,)), ((), ())), preferred_element_type=...]
    all_gather x3 -> x0, waiting for transfers between devices: 23.9 us -> none  [gather(): return lax.all_gather(x, 'expert', axis=0, tiled=True)]
    all_gather x2 -> x0, blocking collectives: 12.4 us -> none  [gather(): return lax.all_gather(x, 'expert', axis=0, tiled=True)]
    ppermute x2 -> x0, starting transfers between devices: 7.11 us -> none  [passed_along(): return lax.ppermute(x, axis, pairs)]
  transfers between devices with their start and end apart: 10 -> 0, of which waited for: 8 -> 0; matrix products, arithmetic and copies ran while one was open for 13% -> 0% of each run, Pallas kernels for 0% -> 0%
where the time goes in v2:
time: 115 us; the launch traced here: 114 us
  Pallas kernels  102 us (89%)
  local copies, waits for them, and re-layouts  8.49 us (7%)
  other arithmetic  3.01 us (3%)
    pallas_call x1, Pallas kernels, shards(): pl.pallas_call(functools.partial(kernel, (sections, replicas, owners)), o...  102 us
    unnamed x10, local copies, waits for them, and re-layouts  5.62 us

profile of v2, /device:TPU:0, one launch (start us, length us, event | category | flops | bytes accessed | tf_op | source)
XLA Modules:
  0.0 114.5 jit_solution(5589340983469649670)
XLA Ops:
  0.6 0.7 convert_bitcast_fusion.1
  1.3 0.7 convert_bitcast_fusion
  2.0 0.1 copy.16
  2.1 0.6 pad.14.lanes_bwd
  2.7 0.1 copy.15
  2.8 0.6 pad.13.lanes_fwd
  3.5 1.6 %pad_convert_fusion = (f32[16,6144]{1,0:T(8,128)}, bf16[16,6144]{1,0:T(8,128)(2,1)}) fusion(bf16[4,6144]{1,0:T(4,128)(2,1)} %bitcast.29), kind=kLoop, calls=%fused_computation | loop fusion | flops 98304 | bytes 638976 | tf_op jit(solution)/shard_map/jit(_pad)/pad | solution.py:518
  5.1 102.3 %relay_step.1 = (bf16[64,6144]{1,0:T(8,128)(2,1)}, bf16[64,6144]{1,0:T(8,128)(2,1)}, bf16[3072,256]{1,0:T(8,128)(2,1)}, bf16[128,3072]{1,0:T(8,128)(2,1)}, f32[16,768]{1,0:T(8,128)}) custom-call(bf16[64,6144]{1,0:T(8,128)(2,1)} %fresh.1, bf16[64,6144]{1,0:T(8,128)(2,1)} %cotangent.1, bf16[64,6144]{1,0:T(8,128)(2,1)} %bitcast.23, bf16[64,6144]{1,0:T(8,128)(2,1)} %bitcast.24, ...), custom_call_target="tpu_custom_call" | custom-call | tf_op jit(solution)/shard_map/relay_step/pallas_call | solution.py:524
  107.4 0.0 copy-start.2
  107.4 1.4 %slice_bitcast_fusion = f32[1,768,4]{1,2,0:T(4,128)} fusion(f32[16,768]{1,0:T(8,128)} %get-tuple-element.14), kind=kLoop, calls=%fused_computation.1 | loop fusion | bytes 24576 | tf_op jit(solution)/shard_map/broadcast_in_dim | solution.py:597
  108.9 0.0 copy-start
  108.9 2.2 %copy.21 = bf16[1,64,6144]{2,1,0:T(8,128)(2,1)} copy(bf16[1,64,6144]{2,1,0:T(8,128)(2,1)} %bitcast.28) | data formatting | bytes 1572864
  111.0 0.0 copy-done.2
  111.0 0.9 copy.22
  111.9 0.0 copy-done
  111.9 0.0 copy-start.1
  111.9 1.1 copy.23
  113.1 0.5 copy-done.1
  113.6 0.9 copy.24
Async XLA Ops:
  107.4 3.6 %copy-start.2 = (bf16[64,6144]{1,0:T(8,128)(2,1)S(1)}, bf16[64,6144]{1,0:T(8,128)(2,1)}, u32[]{:S(2)}) copy-start(bf16[64,6144]{1,0:T(8,128)(2,1)} %get-tuple-element.11) | copy-start | bytes 2359300
  108.9 3.1 %copy-start = (bf16[3072,256]{1,0:T(8,128)(2,1)S(1)}, bf16[3072,256]{1,0:T(8,128)(2,1)}, u32[]{:S(2)}) copy-start(bf16[3072,256]{1,0:T(8,128)(2,1)} %get-tuple-element.12) | copy-start | bytes 4718596
  111.9 1.7 %copy-start.1 = (bf16[128,3072]{1,0:T(8,128)(2,1)S(1)}, bf16[128,3072]{1,0:T(8,128)(2,1)}, u32[]{:S(2)}) copy-start(bf16[128,3072]{1,0:T(8,128)(2,1)} %get-tuple-element.13) | copy-start | bytes 2359300

commit v3 on v2

--- a/solution.py
+++ b/solution.py
@@ -9,7 +9,6 @@
 
 EPSILON = 1e-05
 MESH = pl.DeviceIdType.MESH
-IDS = 16
 STRIP = 16
 
 
@@ -40,11 +39,18 @@
             self.copy(own, i, lax.rem(self.x + i, self.chips) * 2 + self.c).start()
         self.copy(own, 0, self.x * 2 + 1 - self.c).start()
 
+    def crossed(self):
+        for i in range(1, self.chips):
+            self.copy(self.here(i, self.c), i, self.x * 2 + 1 - self.c).wait_recv()
+
+    def pass_on(self):
+        other = self.x * 2 + 1 - self.c
+        for i in range(1, self.chips):
+            self.copy(self.here(i, self.c), self.chips - 1 + i, other).start()
+
     def forward(self):
-        other = self.x * 2 + 1 - self.c
-        for i in range(1, self.chips):
-            self.copy(self.here(i, self.c), i, other).wait_recv()
-            self.copy(self.here(i, self.c), self.chips - 1 + i, other).start()
+        self.crossed()
+        self.pass_on()
 
     def finish(self):
         other = self.x * 2 + 1 - self.c
@@ -125,7 +131,7 @@
 
 def kernel(
     dims,
-    fresh, cotangent, prev_out, prev_grad, saved_in, lanes_fwd, lanes_bwd, router_b, router_f,
+    fresh, cotangent, prev_out, prev_grad, saved_in, ids_bwd, ids_fwd, router_b,
     gate_up, down,
     section_out, input_grad, grad_gate_up, grad_down, grad_router,
     all_bwd, all_fwd, all_up, part, pair_row, cross_row, pair_y, cross_y,
@@ -137,7 +143,8 @@
     sections, replicas, owners = dims
     tokens, model = saved.shape
     width = down_w.shape[0]
-    experts = owners
+    experts = router_b.shape[0]
+    half = tokens // 2
     chips = owners // 2
     total = owners * tokens
     piece = model // replicas
@@ -193,39 +200,54 @@
     def inverse(values):
         return 1.0 / jnp.sqrt(jnp.mean(values * values, axis=1, keepdims=True) + EPSILON)
 
-    def normalize_into(source, target, lanes):
-        def body(at):
+    def normalize_into(source, target, part_at):
+        def step(k, carry):
+            at = pl.multiple_of(part_at * half + k * STRIP, STRIP)
             values = source[pl.ds(at, STRIP), :].astype(jnp.float32)
             rows = pl.ds(pl.multiple_of(me * tokens + at, STRIP), STRIP)
             target[rows, :model] = (values * inverse(values)).astype(jnp.bfloat16)
-            target[rows, model:] = lanes[pl.ds(at, STRIP), :]
-
-        strips(body)
+            return carry
+
+        lax.fori_loop(0, half // STRIP, step, 0)
 
     load_saved.wait()
-    normalize_into(saved, all_bwd, lanes_bwd)
+    spot = lax.broadcasted_iota(jnp.int32, (2, 128), 0)
+    slot = lax.broadcasted_iota(jnp.int32, (2, 128), 1)
+    all_bwd[own_rows, model:] = (
+        dot(ids_bwd[...].astype(jnp.float32), (slot == spot).astype(jnp.float32), 0, 0)
+        + dot(ids_fwd[...].astype(jnp.float32), (slot == spot + 2).astype(jnp.float32), 0, 0)
+    ).astype(jnp.bfloat16)
+    normalize_into(saved, all_bwd, 0)
     pl.semaphore_wait(
         barrier,
         chips + replicas - 1 + jnp.minimum(section, 1) + jnp.minimum(sections - 1 - section, 1),
     )
 
-    send_out = pltpu.make_async_remote_copy(
-        src_ref=prev_out, dst_ref=inputs_fwd, send_sem=pipe_send.at[0], recv_sem=pipe_recv.at[0],
-        device_id={"pipe": lax.rem(section + 1, sections)}, device_id_type=MESH,
-    )
-    send_grad = pltpu.make_async_remote_copy(
-        src_ref=prev_grad, dst_ref=all_up.at[own_rows],
-        send_sem=pipe_send.at[1], recv_sem=pipe_recv.at[1],
-        device_id={"pipe": lax.rem(section + sections - 1, sections)}, device_id_type=MESH,
-    )
+    def relay_out(h):
+        rows = pl.ds(h * half, half)
+        return pltpu.make_async_remote_copy(
+            src_ref=prev_out.at[rows], dst_ref=inputs_fwd.at[rows],
+            send_sem=pipe_send.at[0, h], recv_sem=pipe_recv.at[0, h],
+            device_id={"pipe": lax.rem(section + 1, sections)}, device_id_type=MESH,
+        )
+
+    def relay_grad(h):
+        rows = pl.ds(pl.multiple_of(me * tokens + h * half, half), half)
+        return pltpu.make_async_remote_copy(
+            src_ref=prev_grad.at[pl.ds(h * half, half)], dst_ref=all_up.at[rows],
+            send_sem=pipe_send.at[1, h], recv_sem=pipe_recv.at[1, h],
+            device_id={"pipe": lax.rem(section + sections - 1, sections)}, device_id_type=MESH,
+        )
 
     @pl.when(has_prev)
     def _():
-        send_grad.start()
+        for h in range(2):
+            relay_grad(h).start()
 
     @pl.when(has_next)
     def _():
-        send_out.start()
+        for h in range(2):
+            relay_out(h).start()
 
     @pl.when(jnp.logical_not(has_prev))
     def _():
@@ -238,10 +260,19 @@
     def block_of(ref):
         return lambda j: ref.at[pl.ds(pl.multiple_of(j * tokens, tokens), tokens)]
 
-    gather_bwd = Gather(block_of(all_bwd), g_send.at[0], g_recv.at[0], chips, x, c)
-    gather_up = Gather(block_of(all_up), g_send.at[1], g_recv.at[1], chips, x, c)
-    gather_fwd = Gather(block_of(all_fwd), g_send.at[2], g_recv.at[2], chips, x, c)
-    gather_gate = Gather(lambda j: gates_all.at[j], g_send.at[3], g_recv.at[3], chips, x, c)
+    def halves(ref, a):
+        def view(h):
+            return lambda j: ref.at[pl.ds(pl.multiple_of(j * tokens + h * half, half), half)]
+
+        return [
+            Gather(view(h), g_send.at[2 * a + h], g_recv.at[2 * a + h], chips, x, c)
+            for h in range(2)
+        ]
+
+    gather_bwd = halves(all_bwd, 0)
+    gather_up = halves(all_up, 1)
+    gather_fwd = halves(all_fwd, 2)
+    gather_gate = Gather(lambda j: gates_all.at[j], g_send.at[6], g_recv.at[6], chips, x, c)
     sems = [
         tuple(ref.at[a] for ref in (s_psend, s_precv, s_csend, s_crecv)) for a in range(2)
     ]
@@ -262,10 +293,10 @@
 
         lax.fori_loop(0, model // chunk, step, 0)
 
-    lane = lax.broadcasted_iota(jnp.int32, (total, IDS), 1).astype(jnp.float32)
+    lane = lax.broadcasted_iota(jnp.int32, (total, experts), 1).astype(jnp.float32)
     mine = (lane == me.astype(jnp.float32)).astype(jnp.float32)
 
-    def project(rows_ref):
+    def project(rows_ref, at):
         pre_acc[...] = jnp.zeros_like(pre_acc)
         log_acc[...] = jnp.zeros_like(log_acc)
 
@@ -275,49 +306,59 @@
             log_acc[...] += dot(rows, router_b[:, cols], 1, 1)
 
         chunks(body)
-        ids = rows_ref[:, model:].astype(jnp.float32)
-        one = (lane == ids[:, 0:1]).astype(jnp.float32)
-        two = (lane == ids[:, 1:2]).astype(jnp.float32)
+        ids = all_bwd[:, model:].astype(jnp.float32)
+        one = (lane == ids[:, at : at + 1]).astype(jnp.float32)
+        two = (lane == ids[:, at + 1 : at + 2]).astype(jnp.float32)
         logits = log_acc[...]
         apart = jnp.sum((one - two) * logits, axis=1, keepdims=True)
         first, second = jax.nn.sigmoid(apart), jax.nn.sigmoid(-apart)
         weight = jnp.sum((one * first + two * second) * mine, axis=1, keepdims=True)
         return one, two, first, second, weight, pre_acc[:, :width], pre_acc[:, width:]
 
-    gather_bwd.start()
-
-    @pl.when(has_next)
-    def _():
-        send_grad.wait_recv()
+    gather_bwd[0].start()
+    normalize_into(saved, all_bwd, 1)
+    gather_bwd[1].start()
 
     @pl.when(jnp.logical_not(has_next))
     def _():
         load_cot.wait()
 
-    gather_up.start()
-    gather_bwd.forward()
+    for h in range(2):
+        @pl.when(has_next)
+        def _():
+            relay_grad(h).wait_recv()
+
+        gather_up[h].start()
+        gather_bwd[h].forward()
 
     @pl.when(has_prev)
     def _():
-        send_out.wait_recv()
+        for h in range(2):
+            relay_out(h).wait_recv()
 
     @pl.when(jnp.logical_not(has_prev))
     def _():
         load_fresh.wait()
 
-    normalize_into(inputs_fwd, all_fwd, lanes_fwd)
+    normalize_into(inputs_fwd, all_fwd, 0)
+    normalize_into(inputs_fwd, all_fwd, 1)
     load_gate.wait()
     load_down.wait()
-    gather_bwd.finish()
-    one, two, first, second, weight, gate, up = project(all_bwd)
+    for h in range(2):
+        gather_bwd[h].finish()
+    one, two, first, second, weight, gate, up = project(all_bwd, 0)
     sig = jax.nn.sigmoid(gate)
     active = gate * sig
     hidden = active * up
     hid_weighted[...] = (weight * hidden).astype(jnp.bfloat16)
 
-    gather_up.forward()
-    gather_fwd.start()
-    gather_up.finish()
+    gather_up[0].forward()
+    gather_up[1].crossed()
+    gather_fwd[0].start()
+    gather_fwd[1].start()
+    gather_up[1].pass_on()
+    gather_up[0].finish()
+    gather_up[1].finish()
     hid_acc[...] = jnp.zeros_like(hid_acc)
 
     def up_body(cols):
@@ -387,7 +428,7 @@
     for j in range(1, owners):
         gate_all = gate_all + gates_all[j].astype(jnp.float32)
     logit = (one - two) * (
-        first * second * jnp.sum((one - two) * gate_all[:, :IDS], axis=1, keepdims=True)
+        first * second * jnp.sum((one - two) * gate_all[:, :experts], axis=1, keepdims=True)
     )
     logit_ref[...] = logit
 
@@ -409,10 +450,12 @@
         rt_copy(i).start()
     rt_own[...] = router_part(dp)
 
-    gather_fwd.forward()
-    gather_fwd.finish()
-    gather_bwd.sent()
-    _, _, _, _, weight_f, gate_f, up_f = project(all_fwd)
+    gather_fwd[0].forward()
+    gather_fwd[1].forward()
+    for h in range(2):
+        gather_fwd[h].finish()
+        gather_bwd[h].sent()
+    _, _, _, _, weight_f, gate_f, up_f = project(all_fwd, 2)
     hid_weighted[...] = (weight_f * (gate_f * jax.nn.sigmoid(gate_f) * up_f)).astype(jnp.bfloat16)
 
     def y_body(cols):
@@ -433,7 +476,9 @@
         normed_grad = scatter_row.total(rows)
         steps_here = logit_ref[home, :]
         for j in range(experts):
-            normed_grad = normed_grad + steps_here[:, j : j + 1] * router_f[j : j + 1, :]
+            normed_grad = normed_grad + steps_here[:, j : j + 1] * router_b[j : j + 1, :].astype(
+                jnp.float32
+            )
         inner = jnp.mean(normed_grad * unit, axis=1, keepdims=True)
         input_grad[rows, :] = (
             all_up[home, :].astype(jnp.float32) + (normed_grad - unit * inner) * inv
@@ -474,14 +519,17 @@
 
     @pl.when(has_prev)
     def _():
-        send_grad.wait_send()
+        for h in range(2):
+            relay_grad(h).wait_send()
 
     @pl.when(has_next)
     def _():
-        send_out.wait_send()
-
-    gather_up.sent()
-    gather_fwd.sent()
+        for h in range(2):
+            relay_out(h).wait_send()
+
+    for h in range(2):
+        gather_up[h].sent()
+        gather_fwd[h].sent()
     gather_gate.sent()
     scatter_row.sent()
     scatter_y.sent()
@@ -494,6 +542,24 @@
             return carry
 
         lax.fori_loop(0, steps, drain, 0)
+
+
+def hand_over(*refs):
+    count = (len(refs) - 1) // 2
+    sems = refs[-1]
+    copies = []
+    for a in range(count):
+        rows = refs[a].shape[0]
+        parts = 2 if rows % 32 == 0 else 1
+        for h in range(parts):
+            at = pl.ds(h * (rows // parts), rows // parts)
+            copies.append(
+                pltpu.make_async_copy(refs[a].at[at], refs[count + a].at[at], sems.at[a, h])
+            )
+    for copy in copies:
+        copy.start()
+    for copy in copies:
+        copy.wait()
 
 
 def shards(
@@ -512,14 +578,10 @@
     steps = piece // chunk
     rt_width = piece // owners if (piece // owners) % 128 == 0 else piece
 
-    def lanes(routes):
-        return jnp.pad(routes[0].astype(jnp.bfloat16), ((0, 0), (0, 126)))
-
-    router_f = jnp.pad(router[0].T.astype(jnp.float32), ((0, IDS - experts), (0, 0)))
     bf16, f32 = jnp.bfloat16, jnp.float32
     far = max(replicas - 1, 1)
     dma = pltpu.SemaphoreType.DMA
-    any_spec = pl.BlockSpec(memory_space=pl.ANY)
+    hbm = pl.BlockSpec(memory_space=pltpu.HBM)
     vmem = pl.BlockSpec(memory_space=pltpu.VMEM)
     outs = pl.pallas_call(
         functools.partial(kernel, (sections, replicas, owners)),
@@ -528,13 +590,13 @@
             jax.ShapeDtypeStruct((tokens, model), bf16),
             jax.ShapeDtypeStruct((piece, 2 * width), bf16),
             jax.ShapeDtypeStruct((width, piece), bf16),
-            jax.ShapeDtypeStruct((IDS, rt_width), f32),
+            jax.ShapeDtypeStruct((experts, rt_width), f32),
         ),
-        in_specs=[any_spec] * 5 + [vmem] * 4 + [any_spec] * 2,
+        in_specs=[hbm] * 5 + [vmem] * 3 + [hbm] * 2,
         out_specs=(vmem,) * 5,
         scratch_shapes=[
             pltpu.VMEM((total, model + 128), bf16),
-            pltpu.VMEM((total, model + 128), bf16),
+            pltpu.VMEM((total, model), bf16),
             pltpu.VMEM((total, model), bf16),
             pltpu.VMEM((total, model), bf16),
             pltpu.VMEM((chips, tokens, model), bf16),
@@ -549,21 +611,21 @@
             pltpu.VMEM((far, steps, chunk, 2 * width), bf16),
             pltpu.VMEM((far, steps, width, chunk), bf16),
             pltpu.VMEM((far, steps, width, chunk), bf16),
-            pltpu.VMEM((far, IDS, rt_width), f32),
-            pltpu.VMEM((far, IDS, rt_width), f32),
+            pltpu.VMEM((far, experts, rt_width), f32),
+            pltpu.VMEM((far, experts, rt_width), f32),
             pltpu.VMEM((owners, total, 128), bf16),
             pltpu.VMEM((total, 2 * width), f32),
-            pltpu.VMEM((total, IDS), f32),
+            pltpu.VMEM((total, experts), f32),
             pltpu.VMEM((total, width), f32),
             pltpu.VMEM((total, 2 * width), bf16),
             pltpu.VMEM((total, width), bf16),
-            pltpu.VMEM((total, IDS), f32),
-            pltpu.VMEM((IDS, rt_width), f32),
+            pltpu.VMEM((total, experts), f32),
+            pltpu.VMEM((experts, rt_width), f32),
             dma((5,)),
-            dma((2,)),
-            dma((2,)),
-            dma((4, 2 * chips - 1)),
-            dma((4, 2 * chips - 1)),
+            dma((2, 2)),
+            dma((2, 2)),
+            dma((7, 2 * chips - 1)),
+            dma((7, 2 * chips - 1)),
             dma((2, chips)),
             dma((2, chips)),
             dma((2, chips - 1)),
@@ -576,14 +638,22 @@
             dma((far,)),
         ],
         compiler_params=pltpu.CompilerParams(
-            collective_id=0, has_side_effects=True, vmem_limit_bytes=62 * 2**20
+            collective_id=0, has_side_effects=True, vmem_limit_bytes=60 * 2**20
         ),
         name="relay_step",
     )(
-        fresh, cotangent, prev_out[0], prev_grad[0], saved_in[0], lanes(route_fwd),
-        lanes(route_bwd), router_f.astype(bf16), router_f, gate_up[0, 0], down[0, 0],
+        fresh, cotangent, prev_out[0], prev_grad[0], saved_in[0],
+        route_bwd[0].T, route_fwd[0].T, router[0].T, gate_up[0, 0], down[0, 0],
     )
-    section_out, input_grad, grad_gate_up, grad_down, grad_router = outs
+    section_out, input_grad, grad_gate_up, grad_down, grad_router = pl.pallas_call(
+        hand_over,
+        out_shape=[jax.ShapeDtypeStruct(out.shape, out.dtype) for out in outs],
+        in_specs=[hbm] * 5,
+        out_specs=[hbm] * 5,
+        scratch_shapes=[dma((5, 2))],
+        compiler_params=pltpu.CompilerParams(vmem_limit_bytes=60 * 2**20),
+        name="hand_over",
+    )(*outs)
     share = piece // owners
     if rt_width != share:
         grad_router = lax.dynamic_slice_in_dim(
@@ -594,7 +664,7 @@
         input_grad[None],
         grad_gate_up[None, None],
         grad_down[None, None],
-        grad_router[:experts].T[None],
+        grad_router.T[None],
     )
 
 

time: 115 us -> 223 us (1.94)
  Pallas kernels: 102 us -> 222 us
  local copies, waits for them, and re-layouts: 8.49 us -> 0 us
  other arithmetic: 3.01 us -> 0 us
    pallas_call x0 -> x1, Pallas kernels: none -> 121 us  [shards(): pl.pallas_call(hand_over, out_shape=[jax.ShapeDtypeStruct(out.shape, out....]
    unnamed x10 -> x0, local copies, waits for them, and re-layouts: 5.62 us -> none
where the time goes in v3:
time: 223 us
  Pallas kernels  222 us (100%)
    pallas_call x1, Pallas kernels, shards(): pl.pallas_call(hand_over, out_shape=[jax.ShapeDtypeStruct(out.shape, out....  121 us
    pallas_call x1, Pallas kernels, shards(): pl.pallas_call(functools.partial(kernel, (sections, replicas, owners)), o...  102 us

profile of v3, /device:TPU:0, one launch (start us, length us, event | category | flops | bytes accessed | tf_op | source)
XLA Modules:
  0.0 223.0 jit_solution(1941674246412017214)
XLA Ops:
  0.6 101.7 %relay_step.1 = (bf16[64,6144]{1,0:T(8,128)(2,1)}, bf16[64,6144]{1,0:T(8,128)(2,1)}, bf16[3072,256]{1,0:T(8,128)(2,1)}, bf16[128,3072]{1,0:T(8,128)(2,1)}, f32[4,768]{1,0:T(4,128)}) custom-call(bf16[64,6144]{1,0:T(8,128)(2,1)} %fresh.1, bf16[64,6144]{1,0:T(8,128)(2,1)} %cotangent.1, bf16[64,6144]{1,0:T(8,128)(2,1)} %bitcast.23, bf16[64,6144]{1,0:T(8,128)(2,1)} %bitcast.24, ...), custom_call_target="tpu_custom_call" | custom-call | tf_op jit(solution)/shard_map/relay_step/pallas_call | solution.py:586
  102.3 120.7 %hand_over.1 = (bf16[64,6144]{1,0:T(8,128)(2,1)}, bf16[64,6144]{1,0:T(8,128)(2,1)}, bf16[3072,256]{1,0:T(8,128)(2,1)}, bf16[128,3072]{1,0:T(8,128)(2,1)}, f32[4,768]{1,0:T(4,128)}) custom-call(bf16[64,6144]{1,0:T(8,128)(2,1)} %get-tuple-element.15.refs_0_, bf16[64,6144]{1,0:T(8,128)(2,1)} %get-tuple-element.16.refs_1_, ...), custom_call_target="tpu_custom_call" | custom-call | tf_op jit(solution)/shard_map/hand_over/pallas_call | solution.py:648

commit v4 on v3

--- a/solution.py
+++ b/solution.py
@@ -232,9 +232,9 @@
         )
 
     def relay_grad(h):
-        rows = pl.ds(pl.multiple_of(me * tokens + h * half, half), half)
+        cols = pl.ds(h * (model // 2), model // 2)
         return pltpu.make_async_remote_copy(
-            src_ref=prev_grad.at[pl.ds(h * half, half)], dst_ref=all_up.at[rows],
+            src_ref=prev_grad.at[:, cols], dst_ref=all_up.at[own_rows, cols],
             send_sem=pipe_send.at[1, h], recv_sem=pipe_recv.at[1, h],
             device_id={"pipe": lax.rem(section + sections - 1, sections)}, device_id_type=MESH,
         )
@@ -269,9 +269,19 @@
             for h in range(2)
         ]
 
+    def column_halves(ref, a):
+        def view(h):
+            cols = pl.ds(h * (model // 2), model // 2)
+            return lambda j: ref.at[pl.ds(pl.multiple_of(j * tokens, tokens), tokens), cols]
+
+        return [
+            Gather(view(h), g_send.at[2 * a + h], g_recv.at[2 * a + h], chips, x, c)
+            for h in range(2)
+        ]
+
     gather_bwd = halves(all_bwd, 0)
-    gather_up = halves(all_up, 1)
-    gather_fwd = halves(all_fwd, 2)
+    gather_up = column_halves(all_up, 1)
+    gather_fwd = column_halves(all_fwd, 2)
     gather_gate = Gather(lambda j: gates_all.at[j], g_send.at[6], g_recv.at[6], chips, x, c)
     sems = [
         tuple(ref.at[a] for ref in (s_psend, s_precv, s_csend, s_crecv)) for a in range(2)
@@ -286,17 +296,19 @@
     def columns(k):
         return pl.ds(pl.multiple_of(k * chunk, chunk), chunk)
 
-    def chunks(body):
+    every = model // chunk
+
+    def chunks(body, begin=0, end=every):
         def step(k, carry):
             body(columns(k))
             return carry
 
-        lax.fori_loop(0, model // chunk, step, 0)
+        lax.fori_loop(begin, end, step, 0)
 
     lane = lax.broadcasted_iota(jnp.int32, (total, experts), 1).astype(jnp.float32)
     mine = (lane == me.astype(jnp.float32)).astype(jnp.float32)
 
-    def project(rows_ref, at):
+    def project(rows_ref, at, ready):
         pre_acc[...] = jnp.zeros_like(pre_acc)
         log_acc[...] = jnp.zeros_like(log_acc)
 
@@ -305,7 +317,9 @@
             pre_acc[...] += dot(rows, gate_up_w[cols, :], 1, 0)
             log_acc[...] += dot(rows, router_b[:, cols], 1, 1)
 
-        chunks(body)
+        for h in range(2):
+            ready(h)
+            chunks(body, h * every // 2, (h + 1) * every // 2)
         ids = all_bwd[:, model:].astype(jnp.float32)
         one = (lane == ids[:, at : at + 1]).astype(jnp.float32)
         two = (lane == ids[:, at + 1 : at + 2]).astype(jnp.float32)
@@ -346,7 +360,7 @@
     load_down.wait()
     for h in range(2):
         gather_bwd[h].finish()
-    one, two, first, second, weight, gate, up = project(all_bwd, 0)
+    one, two, first, second, weight, gate, up = project(all_bwd, 0, lambda h: None)
     sig = jax.nn.sigmoid(gate)
     active = gate * sig
     hidden = active * up
@@ -357,14 +371,14 @@
     gather_fwd[0].start()
     gather_fwd[1].start()
     gather_up[1].pass_on()
-    gather_up[0].finish()
-    gather_up[1].finish()
     hid_acc[...] = jnp.zeros_like(hid_acc)
 
     def up_body(cols):
         hid_acc[...] += dot(all_up[:, cols], down_w[:, cols], 1, 1)
 
-    chunks(up_body)
+    for h in range(2):
+        gather_up[h].finish()
+        chunks(up_body, h * every // 2, (h + 1) * every // 2)
     up_down = hid_acc[...]
     gate_grad = jnp.sum(hidden * up_down, axis=1, keepdims=True)
     lanes = lax.broadcasted_iota(jnp.int32, (total, 128), 1).astype(jnp.float32)
@@ -450,12 +464,13 @@
         rt_copy(i).start()
     rt_own[...] = router_part(dp)
 
-    gather_fwd[0].forward()
-    gather_fwd[1].forward()
+    def fwd_ready(h):
+        gather_fwd[h].forward()
+        gather_fwd[h].finish()
+
     for h in range(2):
-        gather_fwd[h].finish()
         gather_bwd[h].sent()
-    _, _, _, _, weight_f, gate_f, up_f = project(all_fwd, 2)
+    _, _, _, _, weight_f, gate_f, up_f = project(all_fwd, 2, fwd_ready)
     hid_weighted[...] = (weight_f * (gate_f * jax.nn.sigmoid(gate_f) * up_f)).astype(jnp.bfloat16)
 
     def y_body(cols):
@@ -545,21 +560,26 @@
 
 
 def hand_over(*refs):
-    count = (len(refs) - 1) // 2
-    sems = refs[-1]
+    sources, targets, stages, arrive, leave = refs[:5], refs[5:10], refs[10:15], refs[15], refs[16]
     copies = []
-    for a in range(count):
-        rows = refs[a].shape[0]
+    for a in range(5):
+        rows = sources[a].shape[0]
         parts = 2 if rows % 32 == 0 else 1
         for h in range(parts):
             at = pl.ds(h * (rows // parts), rows // parts)
             copies.append(
-                pltpu.make_async_copy(refs[a].at[at], refs[count + a].at[at], sems.at[a, h])
+                (
+                    pltpu.make_async_copy(sources[a].at[at], stages[a].at[at], arrive.at[a, h]),
+                    pltpu.make_async_copy(stages[a].at[at], targets[a].at[at], leave.at[a, h]),
+                )
             )
-    for copy in copies:
-        copy.start()
-    for copy in copies:
-        copy.wait()
+    for first, _ in copies:
+        first.start()
+    for first, then in copies:
+        first.wait()
+        then.start()
+    for _, then in copies:
+        then.wait()
 
 
 def shards(
@@ -650,7 +670,8 @@
         out_shape=[jax.ShapeDtypeStruct(out.shape, out.dtype) for out in outs],
         in_specs=[hbm] * 5,
         out_specs=[hbm] * 5,
-        scratch_shapes=[dma((5, 2))],
+        scratch_shapes=[pltpu.VMEM(out.shape, out.dtype) for out in outs]
+        + [dma((5, 2)), dma((5, 2))],
         compiler_params=pltpu.CompilerParams(vmem_limit_bytes=60 * 2**20),
         name="hand_over",
     )(*outs)

time: 223 us -> 105 us (0.47)
  Pallas kernels: 222 us -> 104 us
    pallas_call x1, Pallas kernels: 121 us -> 3.41 us  [shards(): pl.pallas_call(hand_over, out_shape=[jax.ShapeDtypeStruct(out.shape, out....]
where the time goes in v4:
time: 105 us
  Pallas kernels  104 us (99%)
    pallas_call x1, Pallas kernels, shards(): pl.pallas_call(functools.partial(kernel, (sections, replicas, owners)), o...  101 us
    pallas_call x1, Pallas kernels, shards(): pl.pallas_call(hand_over, out_shape=[jax.ShapeDtypeStruct(out.shape, out....  3.41 us

profile of v4, /device:TPU:0, one launch (start us, length us, event | category | flops | bytes accessed | tf_op | source)
XLA Modules:
  0.0 104.7 jit_solution(7387084079572603170)
XLA Ops:
  0.6 100.6 %relay_step.1 = (bf16[64,6144]{1,0:T(8,128)(2,1)}, bf16[64,6144]{1,0:T(8,128)(2,1)}, bf16[3072,256]{1,0:T(8,128)(2,1)}, bf16[128,3072]{1,0:T(8,128)(2,1)}, f32[4,768]{1,0:T(4,128)}) custom-call(bf16[64,6144]{1,0:T(8,128)(2,1)} %fresh.1, bf16[64,6144]{1,0:T(8,128)(2,1)} %cotangent.1, bf16[64,6144]{1,0:T(8,128)(2,1)} %bitcast.23, bf16[64,6144]{1,0:T(8,128)(2,1)} %bitcast.24, ...), custom_call_target="tpu_custom_call" | custom-call | tf_op jit(solution)/shard_map/relay_step/pallas_call | solution.py:606
  101.3 3.4 %hand_over.1 = (bf16[64,6144]{1,0:T(8,128)(2,1)}, bf16[64,6144]{1,0:T(8,128)(2,1)}, bf16[3072,256]{1,0:T(8,128)(2,1)}, bf16[128,3072]{1,0:T(8,128)(2,1)}, f32[4,768]{1,0:T(4,128)}) custom-call(bf16[64,6144]{1,0:T(8,128)(2,1)} %get-tuple-element.15.refs_0_, bf16[64,6144]{1,0:T(8,128)(2,1)} %get-tuple-element.16.refs_1_, ...), custom_call_target="tpu_custom_call" | custom-call | tf_op jit(solution)/shard_map/hand_over/pallas_call | solution.py:668

commit v5 on v4

--- a/solution.py
+++ b/solution.py
@@ -223,6 +223,12 @@
         chips + replicas - 1 + jnp.minimum(section, 1) + jnp.minimum(sections - 1 - section, 1),
     )
 
+    def up_half(h):
+        return lax.rem(dp + 1 + h, 2) if replicas == 2 else h
+
+    def up_columns(h):
+        return pl.ds(pl.multiple_of(up_half(h) * (model // 2), model // 2), model // 2)
+
     def relay_out(h):
         rows = pl.ds(h * half, half)
         return pltpu.make_async_remote_copy(
@@ -232,7 +238,7 @@
         )
 
     def relay_grad(h):
-        cols = pl.ds(h * (model // 2), model // 2)
+        cols = up_columns(h)
         return pltpu.make_async_remote_copy(
             src_ref=prev_grad.at[:, cols], dst_ref=all_up.at[own_rows, cols],
             send_sem=pipe_send.at[1, h], recv_sem=pipe_recv.at[1, h],
@@ -269,9 +275,9 @@
             for h in range(2)
         ]
 
-    def column_halves(ref, a):
+    def column_halves(ref, a, where):
         def view(h):
-            cols = pl.ds(h * (model // 2), model // 2)
+            cols = where(h)
             return lambda j: ref.at[pl.ds(pl.multiple_of(j * tokens, tokens), tokens), cols]
 
         return [
@@ -280,8 +286,8 @@
         ]
 
     gather_bwd = halves(all_bwd, 0)
-    gather_up = column_halves(all_up, 1)
-    gather_fwd = column_halves(all_fwd, 2)
+    gather_up = column_halves(all_up, 1, up_columns)
+    gather_fwd = column_halves(all_fwd, 2, lambda h: pl.ds(h * (model // 2), model // 2))
     gather_gate = Gather(lambda j: gates_all.at[j], g_send.at[6], g_recv.at[6], chips, x, c)
     sems = [
         tuple(ref.at[a] for ref in (s_psend, s_precv, s_csend, s_crecv)) for a in range(2)
@@ -298,12 +304,12 @@
 
     every = model // chunk
 
-    def chunks(body, begin=0, end=every):
+    def chunks(body, begin=0, count=every):
         def step(k, carry):
-            body(columns(k))
+            body(columns(begin + k))
             return carry
 
-        lax.fori_loop(begin, end, step, 0)
+        lax.fori_loop(0, count, step, 0)
 
     lane = lax.broadcasted_iota(jnp.int32, (total, experts), 1).astype(jnp.float32)
     mine = (lane == me.astype(jnp.float32)).astype(jnp.float32)
@@ -319,7 +325,7 @@
 
         for h in range(2):
             ready(h)
-            chunks(body, h * every // 2, (h + 1) * every // 2)
+            chunks(body, h * every // 2, every // 2)
         ids = all_bwd[:, model:].astype(jnp.float32)
         one = (lane == ids[:, at : at + 1]).astype(jnp.float32)
         two = (lane == ids[:, at + 1 : at + 2]).astype(jnp.float32)
@@ -366,19 +372,56 @@
     hidden = active * up
     hid_weighted[...] = (weight * hidden).astype(jnp.bfloat16)
 
+    def gu_copy(i, k):
+        return pltpu.make_async_remote_copy(
+            src_ref=gu_send.at[i - 1, k], dst_ref=gu_recv.at[i - 1, k],
+            send_sem=gu_ss.at[i - 1, k], recv_sem=gu_rs.at[i - 1, k],
+            device_id={"dp": lax.rem(dp + i, replicas)}, device_id_type=MESH,
+        )
+
+    def dn_copy(i, k):
+        return pltpu.make_async_remote_copy(
+            src_ref=dn_send.at[i - 1, k], dst_ref=dn_recv.at[i - 1, k],
+            send_sem=dn_ss.at[i - 1, k], recv_sem=dn_rs.at[i - 1, k],
+            device_id={"dp": lax.rem(dp + i, replicas)}, device_id_type=MESH,
+        )
+
+    def part_columns(owner, k):
+        return pl.ds(pl.multiple_of(owner * piece + k * chunk, chunk), chunk)
+
+    def gate_part(owner, k):
+        cols = part_columns(owner, k)
+        return dot(all_bwd[:, cols], grad_pre[...], 0, 0).astype(jnp.bfloat16)
+
+    def down_part(owner, k):
+        cols = part_columns(owner, k)
+        return dot(hid_weighted[...], all_up[:, cols], 0, 0).astype(jnp.bfloat16)
+
+    def send_down_parts():
+        for i in range(1, replicas):
+            def step(k, carry, i=i):
+                dn_send[i - 1, k] = down_part(lax.rem(dp + i, replicas), k)
+                dn_copy(i, k).start()
+                return carry
+
+            lax.fori_loop(0, steps, step, 0)
+
     gather_up[0].forward()
+    hid_acc[...] = jnp.zeros_like(hid_acc)
+
+    def up_body(cols):
+        hid_acc[...] += dot(all_up[:, cols], down_w[:, cols], 1, 1)
+
+    gather_up[0].finish()
+    if replicas == 2:
+        send_down_parts()
+    chunks(up_body, up_half(0) * (every // 2), every // 2)
     gather_up[1].crossed()
     gather_fwd[0].start()
     gather_fwd[1].start()
     gather_up[1].pass_on()
-    hid_acc[...] = jnp.zeros_like(hid_acc)
-
-    def up_body(cols):
-        hid_acc[...] += dot(all_up[:, cols], down_w[:, cols], 1, 1)
-
-    for h in range(2):
-        gather_up[h].finish()
-        chunks(up_body, h * every // 2, (h + 1) * every // 2)
+    gather_up[1].finish()
+    chunks(up_body, up_half(1) * (every // 2), every // 2)
     up_down = hid_acc[...]
     gate_grad = jnp.sum(hidden * up_down, axis=1, keepdims=True)
     lanes = lax.broadcasted_iota(jnp.int32, (total, 128), 1).astype(jnp.float32)
@@ -390,36 +433,15 @@
     grad_pre[:, :width] = (hidden_grad * up * sig * (1.0 + gate * (1.0 - sig))).astype(jnp.bfloat16)
     grad_pre[:, width:] = (hidden_grad * active).astype(jnp.bfloat16)
 
-    def gu_copy(i, k):
-        return pltpu.make_async_remote_copy(
-            src_ref=gu_send.at[i - 1, k], dst_ref=gu_recv.at[i - 1, k],
-            send_sem=gu_ss.at[i - 1, k], recv_sem=gu_rs.at[i - 1, k],
-            device_id={"dp": lax.rem(dp + i, replicas)}, device_id_type=MESH,
-        )
-
-    def dn_copy(i, k):
-        return pltpu.make_async_remote_copy(
-            src_ref=dn_send.at[i - 1, k], dst_ref=dn_recv.at[i - 1, k],
-            send_sem=dn_ss.at[i - 1, k], recv_sem=dn_rs.at[i - 1, k],
-            device_id={"dp": lax.rem(dp + i, replicas)}, device_id_type=MESH,
-        )
-
-    def weight_parts(owner, k):
-        cols = pl.ds(pl.multiple_of(owner * piece + k * chunk, chunk), chunk)
-        gu = dot(all_bwd[:, cols], grad_pre[...], 0, 0).astype(jnp.bfloat16)
-        dn = dot(hid_weighted[...], all_up[:, cols], 0, 0).astype(jnp.bfloat16)
-        return gu, dn
-
     for i in range(1, replicas):
         def send_step(k, carry, i=i):
-            gu, dn = weight_parts(lax.rem(dp + i, replicas), k)
-            gu_send[i - 1, k] = gu
-            dn_send[i - 1, k] = dn
+            gu_send[i - 1, k] = gate_part(lax.rem(dp + i, replicas), k)
             gu_copy(i, k).start()
-            dn_copy(i, k).start()
             return carry
 
         lax.fori_loop(0, steps, send_step, 0)
+    if replicas != 2:
+        send_down_parts()
 
     def row_body(cols):
         part[:, cols] = dot(grad_pre[...], gate_up_w[cols, :], 1, 1).astype(jnp.bfloat16)
@@ -428,9 +450,8 @@
     scatter_row.start()
 
     def own_step(k, carry):
-        gu, dn = weight_parts(dp, k)
-        grad_gate_up[columns(k), :] = gu
-        grad_down[:, columns(k)] = dn
+        grad_gate_up[columns(k), :] = gate_part(dp, k)
+        grad_down[:, columns(k)] = down_part(dp, k)
         return carry
 
     gather_gate.forward()

time: 105 us -> 101 us (0.962)
  Pallas kernels: 104 us -> 101 us
    pallas_call x1, Pallas kernels: 101 us -> 97.2 us  [shards(): pl.pallas_call(functools.partial(kernel, (sections, replicas, owners)), o...]
where the time goes in v5:
time: 101 us
  Pallas kernels  101 us (100%)
    pallas_call x1, Pallas kernels, shards(): pl.pallas_call(functools.partial(kernel, (sections, replicas, owners)), o...  97.2 us
    pallas_call x1, Pallas kernels, shards(): pl.pallas_call(hand_over, out_shape=[jax.ShapeDtypeStruct(out.shape, out....  3.41 us

profile of v5, /device:TPU:0, one launch (start us, length us, event | category | flops | bytes accessed | tf_op | source)
XLA Modules:
  0.0 101.3 jit_solution(346020782479429894)
XLA Ops:
  0.6 97.2 %relay_step.1 = (bf16[64,6144]{1,0:T(8,128)(2,1)}, bf16[64,6144]{1,0:T(8,128)(2,1)}, bf16[3072,256]{1,0:T(8,128)(2,1)}, bf16[128,3072]{1,0:T(8,128)(2,1)}, f32[4,768]{1,0:T(4,128)}) custom-call(bf16[64,6144]{1,0:T(8,128)(2,1)} %fresh.1, bf16[64,6144]{1,0:T(8,128)(2,1)} %cotangent.1, bf16[64,6144]{1,0:T(8,128)(2,1)} %bitcast.23, bf16[64,6144]{1,0:T(8,128)(2,1)} %bitcast.24, ...), custom_call_target="tpu_custom_call" | custom-call | tf_op jit(solution)/shard_map/relay_step/pallas_call | solution.py:627
  97.8 3.4 %hand_over.1 = (bf16[64,6144]{1,0:T(8,128)(2,1)}, bf16[64,6144]{1,0:T(8,128)(2,1)}, bf16[3072,256]{1,0:T(8,128)(2,1)}, bf16[128,3072]{1,0:T(8,128)(2,1)}, f32[4,768]{1,0:T(4,128)}) custom-call(bf16[64,6144]{1,0:T(8,128)(2,1)} %get-tuple-element.15.refs_0_, bf16[64,6144]{1,0:T(8,128)(2,1)} %get-tuple-element.16.refs_1_, ...), custom_call_target="tpu_custom_call" | custom-call | tf_op jit(solution)/shard_map/hand_over/pallas_call | solution.py:689
